TPU v7x, 32 devices: a whole 2x2x4 slice. The times are simulated.
32 devices in a mesh: band: 2 (over x), tile: 8 (over z, y), bin: 2 (over core).
Axes of the slice: x: 2, y: 2, z: 4, core: 2. Of those that a mesh axis runs over, the one named last changes fastest.
Arguments:
- spectra: float32 [1296, 8192], P(None, ('band', 'tile', 'bin')), parts along dimension 1, may hold values from 0.25 to 2
- wind: float32 [2, 8192], P(None, ('band', 'tile', 'bin')), parts along dimension 1, may hold values from -5 to 5
- mask: int32 [64, 256], P(None, 'band'), parts along dimension 1, may hold values from 0 to 1, as said below
- dia_index: int32 [2, 2, 4, 1296], replicated, may hold values from 0 to 1295, as said below
- dia_weight: bfloat16 [2, 2, 4, 1296], replicated, may hold values from 0.099609375 to 0.5
- nl_coef: float32 [1296], replicated, may hold values from 0.01 to 0.1
Outputs:
- propagated: float32 [1296, 64, 256], P('bin', 'tile', 'band'), parts along dimension 2
There are 2 independent parts, one for each index of `band`. A program takes and returns all parts, laid end to end along the dimension named above; an argument that names none is the same for every part. Nothing has to cross between parts.
Inputs may be any that keep to these rules, and one draw needn't show every extreme that they name: `mask`: exactly 4096 cells are sea; at least one tile of 8 columns is entirely sea. `dia_index`: for each mirror, member and bin, the corners are frequencies f and f + 1 with f in 0..34 and directions d and d + 1 modulo 36: four different bins.
All inputs are finite; a program needn't handle non-finite values.
Results may differ from a plain program's by a relative error of at most 0.0011.
Values sent between devices are 32-bit elements; how exact they have to be, the bound alone decides.
No kernel may reach another device: no remote copies, remote signals or barrier semaphores. Data moves between devices by JAX's collectives and lax.ppermute only.
A program may use at most 128 MiB of HBM per device.

v0:
```python
import math

import jax
import jax.numpy as jnp
from jax import lax
from jax.sharding import PartitionSpec as P

NTH = 36
STEPS = 2


LAMBDA = 0.25
COEF_THREE = (1.0 + LAMBDA) ** (-4)
COEF_FOUR = (1.0 - LAMBDA) ** (-4)
COEF_BOTH = (1.0 - LAMBDA * LAMBDA) ** (-4)
CFL_LIMIT = 0.8
WIND_RATE = 0.2


def with_halo(block, sides, width):
    for axis, dim in sides:
        count = lax.axis_size(axis)
        forward = [(i, i + 1) for i in range(count - 1)]
        forward.append((count - 1, 0))
        backward = [(target, source) for source, target in forward]
        low = lax.ppermute(
            lax.slice_in_dim(block, block.shape[dim] - width, None, axis=dim), axis, forward
        )
        high = lax.ppermute(lax.slice_in_dim(block, 0, width, axis=dim), axis, backward)
        block = jnp.concatenate([low, block, high], axis=dim)
    return block


def bin_tables(count_bins):
    bin_range = jnp.arange(count_bins)
    theta = 2.0 * math.pi * (bin_range % NTH).astype(jnp.float32) / NTH
    group_speed = CFL_LIMIT * 1.1 ** (-(bin_range // NTH).astype(jnp.float32))
    return (jnp.cos(theta), jnp.sin(theta), group_speed)


def onehot_matrix(table, weight, bin_range):
    accumulated = jnp.zeros((bin_range.shape[0], bin_range.shape[0]), jnp.bfloat16)
    for corner in range(4):
        accumulated = accumulated + jnp.where(
            table[corner][:, None] == bin_range[None, :],
            weight[corner][:, None],
            jnp.zeros((), jnp.bfloat16),
        )
    return accumulated


def transpose_product(matrix, values):
    return lax.dot_general(
        matrix, values, (((0,), (0,)), ((), ())), preferred_element_type=jnp.float32
    )


def coupling(spectra, third_member, fourth_member, nl_coef):
    return nl_coef[:, None] * (
        spectra * spectra * (COEF_THREE * third_member + COEF_FOUR * fourth_member)
        - 2.0 * COEF_BOTH * spectra * third_member * fourth_member
    )


def upwind(padded, courant, axis, length):

    def window(offset, amount):
        return lax.slice_in_dim(padded, offset, offset + amount, axis=axis)

    faces = length + 1
    left_two = window(0, faces)
    left_one = window(1, faces)
    right_one = window(2, faces)
    right_two = window(3, faces)
    curvature = jnp.where(
        courant >= 0.0,
        right_one - 2.0 * left_one + left_two,
        right_two - 2.0 * right_one + left_one,
    )
    face_value = (
        0.5 * (left_one + right_one)
        - 0.5 * courant * (right_one - left_one)
        - (1.0 - courant * courant) / 6.0 * curvature
    )
    face_flux = courant * face_value
    centre = window(2, length)
    return centre - (
        lax.slice_in_dim(face_flux, 1, faces, axis=axis)
        - lax.slice_in_dim(face_flux, 0, length, axis=axis)
    )


def shards(spectra, wind, mask, dia_index, dia_weight, nl_coef):
    count_bins = spectra.shape[0]
    points = spectra.shape[1]
    group_size = lax.axis_size(("tile", "bin"))
    tile_count = lax.axis_size("tile")
    halves = lax.axis_size("bin")
    half_bins = count_bins // halves
    columns = mask.shape[0] // tile_count
    latitudes = mask.shape[1]
    tile_cells = columns * latitudes
    slots = tile_cells // group_size
    device_rank = lax.axis_index(("tile", "bin"))
    tile_rank = lax.axis_index("tile")
    bin_rank = lax.axis_index("bin")
    rounded = spectra.astype(jnp.bfloat16)
    nonlinear = jnp.zeros(spectra.shape, jnp.float32)
    bin_range = jnp.arange(count_bins)
    for mirror in range(2):
        third_matrix = onehot_matrix(dia_index[mirror, 0], dia_weight[mirror, 0], bin_range)
        fourth_matrix = onehot_matrix(dia_index[mirror, 1], dia_weight[mirror, 1], bin_range)
        third_member = jnp.dot(third_matrix, rounded, preferred_element_type=jnp.float32)
        fourth_member = jnp.dot(fourth_matrix, rounded, preferred_element_type=jnp.float32)
        interaction = coupling(spectra, third_member, fourth_member, nl_coef)
        interaction_low = interaction.astype(jnp.bfloat16)
        nonlinear = (
            nonlinear
            - 2.0 * interaction
            + transpose_product(third_matrix, interaction_low)
            + transpose_product(fourth_matrix, interaction_low)
        )
    cosine, sine_theta, group_speed = bin_tables(count_bins)
    wind_drive = jnp.maximum(
        wind[0][None, :] * cosine[:, None] + wind[1][None, :] * sine_theta[:, None], 0.0
    )
    relaxed = spectra + nonlinear + WIND_RATE * wind_drive * spectra
    flat_mask = mask.reshape(-1)
    sea_rank = jnp.cumsum(flat_mask) - 1
    mine = (flat_mask == 1) & (sea_rank % group_size == device_rank)
    targets = jnp.where(mine, sea_rank // group_size, points)
    cell_of = (
        jnp.zeros((points,), jnp.int32)
        .at[targets]
        .set(jnp.arange(flat_mask.shape[0], dtype=jnp.int32), mode="drop")
    )
    point_tile = cell_of // tile_cells
    tile_range = jnp.arange(tile_count)
    before = jnp.sum((point_tile[None, :] < tile_range[:, None]).astype(jnp.int32), axis=1)
    slot_index = jnp.arange(points) - jnp.sum(
        jnp.where(point_tile[:, None] == tile_range[None, :], before[None, :], 0), axis=1
    )
    outgoing = jnp.transpose(relaxed).reshape(points, halves, half_bins)
    send_values = (
        jnp.zeros((tile_count, halves, slots, half_bins), jnp.float32)
        .at[point_tile, :, slot_index, :]
        .set(outgoing)
    )
    send_cells = (
        jnp.full((tile_count, halves, slots), -1, jnp.int32)
        .at[point_tile, :, slot_index]
        .set(jnp.broadcast_to(cell_of[:, None], (points, halves)))
    )
    got_values, got_cells = (
        lax.all_to_all(
            send_values.reshape(group_size, slots * half_bins),
            ("tile", "bin"),
            split_axis=0,
            concat_axis=0,
            tiled=True,
        ),
        lax.all_to_all(
            send_cells.reshape(group_size, slots),
            ("tile", "bin"),
            split_axis=0,
            concat_axis=0,
            tiled=True,
        ),
    )
    got_values = got_values.reshape(group_size * slots, half_bins)
    got_cells = got_cells.reshape(group_size * slots)
    local_cell = jnp.where(got_cells >= 0, got_cells - tile_rank * tile_cells, tile_cells)
    spectra_grid = (
        jnp.zeros((half_bins, tile_cells), jnp.float32)
        .at[:, local_cell]
        .set(jnp.transpose(got_values), mode="drop")
    )
    spectra_grid = spectra_grid.reshape(half_bins, columns, latitudes)
    courant_x = lax.dynamic_slice_in_dim(group_speed * cosine, bin_rank * half_bins, half_bins, 0)[
        :, None, None
    ]
    courant_y = lax.dynamic_slice_in_dim(
        group_speed * sine_theta, bin_rank * half_bins, half_bins, 0
    )[:, None, None]
    sea_factor = lax.dynamic_slice_in_dim(mask, tile_rank * columns, columns, 0).astype(jnp.float32)
    for substep in range(STEPS):
        padded = with_halo(spectra_grid, (("tile", 1),), 2)
        spectra_grid = upwind(padded, courant_x, 1, columns) * sea_factor
        padded = jnp.pad(spectra_grid, ((0, 0), (0, 0), (2, 2)))
        spectra_grid = upwind(padded, courant_y, 2, latitudes) * sea_factor
    return spectra_grid


def solution(mesh):
    in_specs = (
        P(None, ("band", "tile", "bin")),
        P(None, ("band", "tile", "bin")),
        P(None, "band"),
        P(),
        P(),
        P(),
    )
    out_specs = P("bin", "tile", "band")
    return jax.shard_map(shards, mesh=mesh, in_specs=in_specs, out_specs=out_specs, check_vma=False)
```

profile of v0, /device:TPU:0, one launch (start us, length us, event | category | flops | bytes accessed | tf_op | source)
XLA Modules:
  0.0 296.0 jit_solution(9160287315364788537)
XLA Ops:
  0.0 0.9 compare_bitcast_fusion
  0.9 1.0 reduce-window.9
  2.0 0.1 reduce-window.12
  2.1 0.1 slice_reduce_fusion
  2.3 0.3 compare_select_fusion
  2.6 30.4 %scatter_custom_fusion = s32[256]{0:T(256)S(1)} fusion(s32[8192]{0:T(1024)S(1)} %bitcast.36, s32[8192]{0:T(1024)S(1)} %iota.35, s32[]{:T(128)} %constant.50.clone.1), kind=kCustom, calls=%fused_computation.218 | custom fusion | bytes 1028 | tf_op jit(solution)/shard_map/scatter | solution.py:135
  33.1 0.1 convert_reduce_fusion
  33.4 12.5 %scatter_fusion = s32[8,2,64]{1,2,0:T(8,128)S(1)} fusion(s32[8,2,64]{1,2,0:T(8,128)S(1)} %broadcast_in_dim.233, s32[256]{0:T(256)S(1)} %bitcast.31, s32[256,2]{1,0:T(8,128)S(1)} %broadcast_in_dim.238), kind=kCustom, calls=%fused_computation.1 | custom fusion | bytes 8192 | tf_op jit(solution)/shard_map/scatter | solution.py:152
  46.0 0.7 copy.32
  46.7 7.6 %all-to-all-start = ((s32[16,1,64]{2,1,0:T(1,128)}), s32[16,1,64]{2,1,0:T(1,128)S(1)}, u32[]{:S(2)}, u32[]{:S(2)}) async-start(s32[16,1,64]{2,1,0:T(1,128)} %bitcast.6), calls=%async_computation | async-start | bytes 16384 | tf_op jit(solution)/shard_map/all_to_all | solution.py:162
  54.4 0.2 slice_reduce_fusion.7
  54.7 0.2 slice_reduce_fusion.8
  54.9 4.0 %fusion.80 = f32[1296,256]{1,0:T(8,128)S(1)} fusion(s32[1296]{0:T(1024)S(1)} %get-tuple-element.15, s32[1296]{0:T(1024)S(1)} %get-tuple-element.16, s32[1296]{0:T(1024)S(1)} %get-tuple-element.17, s32[1296]{0:T(1024)S(1)} %get-tuple-element.18, bf16[1296]{0:T(1024)(128)(2,1)S(1)} %get-tuple-element.31, bf16[1296]{0:T(1024)(128)(2,1)S(1)} %get-tuple-element.32, ...), kind=kOutput, calls=%fused_computation.123 | convolution fusion | flops 887169024 | bytes 2685312 | tf_op jit(solution)/shard_map/dot_general | solution.py:113
  59.0 4.5 %subtract_multiply_fusion.1 = f32[1296,256]{1,0:T(8,128)S(1)} fusion(f32[1296,256]{1,0:T(8,128)S(1)} %fusion.80, s32[1296]{0:T(1024)S(1)} %get-tuple-element.11, s32[1296]{0:T(1024)S(1)} %get-tuple-element.12, s32[1296]{0:T(1024)S(1)} %get-tuple-element.13, s32[1296]{0:T(1024)S(1)} %get-tuple-element.14, bf16[1296]{0:T(1024)(128)(2,1)S(1)} %get-tuple-element.27, ...), kind=kOutput, calls=%fused_computation.126 | convolution fusion | flops 890486784 | bytes 4017600 | tf_op jit(solution)/shard_map/dot_general | solution.py:114
  63.5 5.1 %convolution_add_fusion.3 = f32[1296,256]{1,0:T(8,128)S(1)} fusion(s32[1296]{0:T(1024)S(1)} %get-tuple-element.15, s32[1296]{0:T(1024)S(1)} %get-tuple-element.16, s32[1296]{0:T(1024)S(1)} %get-tuple-element.17, s32[1296]{0:T(1024)S(1)} %get-tuple-element.18, bf16[1296]{0:T(1024)(128)(2,1)S(1)} %get-tuple-element.31, ...), kind=kOutput, calls=%fused_computation.106 | convolution fusion | flops 888164352 | bytes 2685312 | tf_op jit(solution)/shard_map/dot_general | solution.py:53
  68.6 4.0 %fusion.83 = f32[1296,256]{1,0:T(8,128)S(1)} fusion(s32[1296]{0:T(1024)S(1)} %get-tuple-element.7, s32[1296]{0:T(1024)S(1)} %get-tuple-element.8, s32[1296]{0:T(1024)S(1)} %get-tuple-element.9, s32[1296]{0:T(1024)S(1)} %get-tuple-element.10, bf16[1296]{0:T(1024)(128)(2,1)S(1)} %get-tuple-element.23, bf16[1296]{0:T(1024)(128)(2,1)S(1)} %get-tuple-element.24, ...), kind=kOutput, calls=%fused_computation.124 | convolution fusion | flops 887169024 | bytes 2685312 | tf_op jit(solution)/shard_map/dot_general | solution.py:113
  72.6 4.5 %subtract_multiply_fusion = f32[1296,256]{1,0:T(8,128)S(1)} fusion(f32[1296,256]{1,0:T(8,128)S(1)} %fusion.83, s32[1296]{0:T(1024)S(1)} %get-tuple-element.19, s32[1296]{0:T(1024)S(1)} %get-tuple-element.20, s32[1296]{0:T(1024)S(1)} %get-tuple-element.6, s32[1296]{0:T(1024)S(1)} %get-tuple-element.5, bf16[1296]{0:T(1024)(128)(2,1)S(1)} %get-tuple-element.35, ...), kind=kOutput, calls=%fused_computation.125 | convolution fusion | flops 890486784 | bytes 4017600 | tf_op jit(solution)/shard_map/dot_general | solution.py:114
  77.1 4.8 %fusion.62 = f32[1296,256]{1,0:T(8,128)S(1)} fusion(f32[1296,256]{1,0:T(8,128)S(1)} %convolution_add_fusion.3, s32[1296]{0:T(1024)S(1)} %get-tuple-element.11, s32[1296]{0:T(1024)S(1)} %get-tuple-element.12, s32[1296]{0:T(1024)S(1)} %get-tuple-element.13, s32[1296]{0:T(1024)S(1)} %get-tuple-element.14, bf16[1296]{0:T(1024)(128)(2,1)S(1)} %get-tuple-element.27, ...), kind=kOutput, calls=%fused_computation.105 | convolution fusion | flops 888164352 | bytes 5339520 | tf_op jit(solution)/shard_map/dot_general | solution.py:53
  81.9 4.7 %convolution_add_fusion.1 = f32[1296,256]{1,0:T(8,128)S(1)} fusion(f32[1296,256]{1,0:T(8,128)S(1)} %fusion.62, s32[1296]{0:T(1024)S(1)} %get-tuple-element.7, s32[1296]{0:T(1024)S(1)} %get-tuple-element.8, s32[1296]{0:T(1024)S(1)} %get-tuple-element.9, s32[1296]{0:T(1024)S(1)} %get-tuple-element.10, bf16[1296]{0:T(1024)(128)(2,1)S(1)} %get-tuple-element.23, ...), kind=kOutput, calls=%fused_computation.103 | convolution fusion | flops 887500800 | bytes 4012416 | tf_op jit(solution)/shard_map/dot_general | solution.py:53
  86.6 5.0 %fusion.61 = f32[1296,256]{1,0:T(8,128)S(1)} fusion(f32[1296,256]{1,0:T(8,128)S(1)} %copy-done.3, f32[1296,256]{1,0:T(8,128)S(1)} %convolution_add_fusion.1, s32[1296]{0:T(1024)S(1)} %get-tuple-element.19, s32[1296]{0:T(1024)S(1)} %get-tuple-element.20, s32[1296]{0:T(1024)S(1)} %get-tuple-element.6, s32[1296]{0:T(1024)S(1)} %get-tuple-element.5, ...), kind=kOutput, calls=%fused_computation.102 | convolution fusion | flops 890155008 | bytes 5351936 | tf_op jit(solution)/shard_map/dot_general | solution.py:53
  91.7 2.1 copy.34
  93.8 0.8 broadcast_in_dim.241
  94.6 24.0 %scatter_fusion.1 = f32[8,2,64,648]{3,1,2,0:T(2,128)S(1)} fusion(f32[8,2,64,648]{3,1,2,0:T(2,128)S(1)} %broadcast_in_dim.241, s32[256]{0:T(256)S(1)} %bitcast.32, f32[256,2,648]{2,1,0:T(2,128)} %copy.34), kind=kCustom, calls=%fused_computation.2 | custom fusion | bytes 3983360 | tf_op jit(solution)/shard_map/scatter | solution.py:147
  118.6 2.0 copy.35
  120.6 7.1 %all_to_all.16 = f32[16,1,41472]{2,1,0:T(1,128)} reshape(f32[8,2,64,648]{3,2,1,0:T(8,128)} %copy.35) | data formatting | bytes 5308416 | tf_op jit(solution)/shard_map/all_to_all | solution.py:155
  127.8 6.0 %all-to-all-start.1 = ((f32[16,1,41472]{2,1,0:T(1,128)}), f32[16,1,41472]{2,1,0:T(1,128)S(1)}, u32[]{:S(2)}, u32[]{:S(2)}) async-start(f32[16,1,41472]{2,1,0:T(1,128)} %all_to_all.16), calls=%async_computation.1 | async-start | bytes 5308416 | tf_op jit(solution)/shard_map/all_to_all | solution.py:155
  133.9 50.7 %all-to-all-done.1 = f32[16,1,41472]{2,1,0:T(1,128)S(1)} async-done(((f32[16,1,41472]{2,1,0:T(1,128)}), f32[16,1,41472]{2,1,0:T(1,128)S(1)}, u32[]{:S(2)}, u32[]{:S(2)}) %all-to-all-start.1) | async-done | bytes 2654240 | tf_op jit(solution)/shard_map/all_to_all | solution.py:155
  184.6 8.6 %reduce.34 = f32[16,41472]{1,0:T(8,128)} reduce(f32[16,1,41472]{2,1,0:T(1,128)S(1)} %all-to-all-done.1, f32[]{:T(128)} %constant.202), dimensions={1}, to_apply=%all_to_all.15.reduce_sub_computation | reduce | bytes 5308420 | tf_op jit(solution)/shard_map/all_to_all | solution.py:155
  193.2 4.7 %reshape.344 = f32[1024,648]{1,0:T(8,128)S(1)} reshape(f32[16,41472]{1,0:T(8,128)} %reduce.34) | data formatting | bytes 5308416 | tf_op jit(solution)/shard_map/reshape | solution.py:170
  197.9 6.6 %scatter_custom_fusion.3 = f32[648,1024]{0,1:T(8,128)} fusion(s32[1024]{0:T(1024)S(1)} %bitcast.39, f32[1024,648]{1,0:T(8,128)S(1)} %reshape.344, f32[]{:T(128)} %constant.45.clone.1), kind=kCustom, calls=%fused_computation.119 | custom fusion | bytes 2654212 | tf_op jit(solution)/shard_map/scatter | solution.py:176
  204.5 2.6 copy.41
  207.2 4.2 %collective-permute-start = (f32[648,2,128]{2,0,1:T(8,128)S(1)}, f32[648,2,128]{2,0,1:T(8,128)S(1)}, u32[]{:S(2)}, u32[]{:S(2)}) collective-permute-start(f32[648,2,128]{2,0,1:T(8,128)S(1)} %get-tuple-element.45), channel_id=1, source_target_pairs={{0,2},{2,4},{4,6},{6,8},{8,10},{10,12},{12,14},{14,0},{1,3},{3,5},... | collective-permute-start | bytes 1990664 | tf_op jit(solution)/shard_map/ppermute | solution.py:26
  211.4 8.0 %collective-permute-start.1 = (f32[648,2,128]{2,0,1:T(8,128)S(1)}, f32[648,2,128]{2,0,1:T(8,128)S(1)}, u32[]{:S(2)}, u32[]{:S(2)}) collective-permute-start(f32[648,2,128]{2,0,1:T(8,128)S(1)} %get-tuple-element.46), channel_id=1, source_target_pairs={{2,0},{4,2},{6,4},{8,6},{10,8},{12,10},{14,12},{0,14},{3,1},{5,3},... | collective-permute-start | bytes 1990664 | tf_op jit(solution)/shard_map/ppermute | solution.py:29
  219.4 0.7 dynamic-slice_convert_fusion
  220.2 20.5 %collective-permute-done = f32[648,2,128]{2,0,1:T(8,128)S(1)} collective-permute-done((f32[648,2,128]{2,0,1:T(8,128)S(1)}, f32[648,2,128]{2,0,1:T(8,128)S(1)}, u32[]{:S(2)}, u32[]{:S(2)}) %collective-permute-start) | collective-permute-done | bytes 663584 | tf_op jit(solution)/shard_map/ppermute | solution.py:26
  240.7 5.6 %collective-permute-done.1 = f32[648,2,128]{2,0,1:T(8,128)S(1)} collective-permute-done((f32[648,2,128]{2,0,1:T(8,128)S(1)}, f32[648,2,128]{2,0,1:T(8,128)S(1)}, u32[]{:S(2)}, u32[]{:S(2)}) %collective-permute-start.1) | collective-permute-done | bytes 663584 | tf_op jit(solution)/shard_map/ppermute | solution.py:29
  246.3 2.0 fusion.58
  248.4 0.3 fusion.70
  248.7 4.4 %fusion.20 = f32[648,8,129]{2,0,1:T(8,128)S(1)} fusion(f32[648,8,128]{2,0,1:T(8,128)S(1)} %fusion.70, f32[648]{0:T(1024)S(1)} %get-tuple-element.50, f32[648]{0:T(1024)S(1)} %get-tuple-element.49, f32[648]{0:T(1024)S(1)} %get-tuple-element.38, pred[648]{0:T(1024)(128)(4,1)S(1)} %get-tuple-element.37), kind=kLoop, calls=%fused_computation.48 | loop fusion | flops 10031040 | bytes 5337576 | tf_op jit(solution)/shard_map/mul | solution.py:85
  253.1 0.8 fusion.68
  254.0 4.7 %collective-permute-start.3 = (f32[648,2,128]{2,0,1:T(8,128)S(1)}, f32[648,2,128]{2,0,1:T(8,128)S(1)}, u32[]{:S(2)}, u32[]{:S(2)}) collective-permute-start(f32[648,2,128]{2,0,1:T(8,128)S(1)} %get-tuple-element.44), channel_id=1, source_target_pairs={{2,0},{4,2},{6,4},{8,6},{10,8},{12,10},{14,12},{0,14},{3,1},{5,3},... | collective-permute-start | bytes 1990664 | tf_op jit(solution)/shard_map/ppermute | solution.py:29
  258.7 22.9 %collective-permute-done.2 = f32[648,2,128]{2,0,1:T(8,128)S(1)} collective-permute-done((f32[648,2,128]{2,0,1:T(8,128)S(1)}, f32[648,2,128]{2,0,1:T(8,128)S(1)}, u32[]{:S(2)}, u32[]{:S(2)}) %collective-permute-start.2) | collective-permute-done | bytes 663584 | tf_op jit(solution)/shard_map/ppermute | solution.py:26
  281.6 4.4 %collective-permute-done.3 = f32[648,2,128]{2,0,1:T(8,128)S(1)} collective-permute-done((f32[648,2,128]{2,0,1:T(8,128)S(1)}, f32[648,2,128]{2,0,1:T(8,128)S(1)}, u32[]{:S(2)}, u32[]{:S(2)}) %collective-permute-start.3) | collective-permute-done | bytes 663584 | tf_op jit(solution)/shard_map/ppermute | solution.py:29
  285.9 2.0 fusion.51
  288.0 0.4 fusion.66
  288.4 4.4 %fusion.27 = f32[648,8,129]{2,0,1:T(8,128)S(1)} fusion(f32[648,8,128]{2,0,1:T(8,128)S(1)} %fusion.66, f32[648]{0:T(1024)S(1)} %get-tuple-element.50, f32[648]{0:T(1024)S(1)} %get-tuple-element.49, f32[648]{0:T(1024)S(1)} %get-tuple-element.38, pred[648]{0:T(1024)(128)(4,1)S(1)} %get-tuple-element.37), kind=kLoop, calls=%fused_computation.55 | loop fusion | flops 10031040 | bytes 5337576 | tf_op jit(solution)/shard_map/mul | solution.py:85
  292.8 0.8 fusion.64
  293.6 2.0 copy.42
  (31 shorter events, 0.9 us)
Async XLA Ops:
  0.0 54.4 %copy-start.2 = (f32[2,256]{1,0:T(2,128)S(1)}, f32[2,256]{1,0:T(2,128)}, u32[]{:S(2)}) copy-start(f32[2,256]{1,0:T(2,128)} %param.7) | copy-start | bytes 6148
  0.0 54.4 %copy-start = (bf16[2,2,4,1296]{3,2,1,0:T(4,128)(2,1)S(1)}, bf16[2,2,4,1296]{3,2,1,0:T(4,128)(2,1)}, u32[]{:S(2)}) copy-start(bf16[2,2,4,1296]{3,2,1,0:T(4,128)(2,1)} %param.10) | copy-start | bytes 124420
  0.0 54.7 %copy-start.1 = (s32[2,2,4,1296]{3,2,1,0:T(4,128)S(1)}, s32[2,2,4,1296]{3,2,1,0:T(4,128)}, u32[]{:S(2)}) copy-start(s32[2,2,4,1296]{3,2,1,0:T(4,128)} %param.9) | copy-start | bytes 248836
  0.0 54.9 %copy-start.3 = (f32[1296,256]{1,0:T(8,128)S(1)}, f32[1296,256]{1,0:T(8,128)}, u32[]{:S(2)}) copy-start(f32[1296,256]{1,0:T(8,128)} %param.6) | copy-start | bytes 3981316
  46.7 81.1 %all-to-all-start = ((s32[16,1,64]{2,1,0:T(1,128)}), s32[16,1,64]{2,1,0:T(1,128)S(1)}, u32[]{:S(2)}, u32[]{:S(2)}) async-start(s32[16,1,64]{2,1,0:T(1,128)} %bitcast.6), calls=%async_computation | async-start | bytes 16384 | tf_op jit(solution)/shard_map/all_to_all | solution.py:162
  54.9 4.1 %copy-start.4 = (f32[1296]{0:T(1024)S(1)}, f32[1296]{0:T(1024)}, u32[]{:S(2)}) copy-start(f32[1296]{0:T(1024)} %param.11) | copy-start | bytes 15556
  127.8 56.8 %all-to-all-start.1 = ((f32[16,1,41472]{2,1,0:T(1,128)}), f32[16,1,41472]{2,1,0:T(1,128)S(1)}, u32[]{:S(2)}, u32[]{:S(2)}) async-start(f32[16,1,41472]{2,1,0:T(1,128)} %all_to_all.16), calls=%async_computation.1 | async-start | bytes 5308416 | tf_op jit(solution)/shard_map/all_to_all | solution.py:155
  207.2 33.5 %collective-permute-start = (f32[648,2,128]{2,0,1:T(8,128)S(1)}, f32[648,2,128]{2,0,1:T(8,128)S(1)}, u32[]{:S(2)}, u32[]{:S(2)}) collective-permute-start(f32[648,2,128]{2,0,1:T(8,128)S(1)} %get-tuple-element.45), channel_id=1, source_target_pairs={{0,2},{2,4},{4,6},{6,8},{8,10},{10,12},{12,14},{14,0},{1,3},{3,5},... | collective-permute-start | bytes 1990664 | tf_op jit(solution)/shard_map/ppermute | solution.py:26
  211.4 34.9 %collective-permute-start.1 = (f32[648,2,128]{2,0,1:T(8,128)S(1)}, f32[648,2,128]{2,0,1:T(8,128)S(1)}, u32[]{:S(2)}, u32[]{:S(2)}) collective-permute-start(f32[648,2,128]{2,0,1:T(8,128)S(1)} %get-tuple-element.46), channel_id=1, source_target_pairs={{2,0},{4,2},{6,4},{8,6},{10,8},{12,10},{14,12},{0,14},{3,1},{5,3},... | collective-permute-start | bytes 1990664 | tf_op jit(solution)/shard_map/ppermute | solution.py:29
  253.9 27.6 %collective-permute-start.2 = (f32[648,2,128]{2,0,1:T(8,128)S(1)}, f32[648,2,128]{2,0,1:T(8,128)S(1)}, u32[]{:S(2)}, u32[]{:S(2)}) collective-permute-start(f32[648,2,128]{2,0,1:T(8,128)S(1)} %get-tuple-element.43), channel_id=1, source_target_pairs={{0,2},{2,4},{4,6},{6,8},{8,10},{10,12},{12,14},{14,0},{1,3},{3,5},... | collective-permute-start | bytes 1990664 | tf_op jit(solution)/shard_map/ppermute | solution.py:26
  254.0 31.9 %collective-permute-start.3 = (f32[648,2,128]{2,0,1:T(8,128)S(1)}, f32[648,2,128]{2,0,1:T(8,128)S(1)}, u32[]{:S(2)}, u32[]{:S(2)}) collective-permute-start(f32[648,2,128]{2,0,1:T(8,128)S(1)} %get-tuple-element.44), channel_id=1, source_target_pairs={{2,0},{4,2},{6,4},{8,6},{10,8},{12,10},{14,12},{0,14},{3,1},{5,3},... | collective-permute-start | bytes 1990664 | tf_op jit(solution)/shard_map/ppermute | solution.py:29
where the time goes:
time: 300 us; the launch traced here: 296 us
  waiting for transfers between devices  104 us (35%)
  local copies, waits for them, and re-layouts  96.8 us (32%)
  matrix products  36.6 us (12%)
  starting transfers between devices  30.6 us (10%)
  other arithmetic  27.3 us (9%)
    all_to_all x1, waiting for transfers between devices, shards(): lax.all_to_all(send_values.reshape(group_size, slots * half_bins), ('tile...  50.7 us
    ppermute x2, waiting for transfers between devices, with_halo(): lax.ppermute(lax.slice_in_dim(block, block.shape[dim] - width, None, axis...  43.4 us
    scatter x1, local copies, waits for them, and re-layouts, shards(): cell_of = jnp.zeros((points,), jnp.int32).at[targets].set(jnp.arange(flat...  30.4 us
    scatter x2, local copies, waits for them, and re-layouts, shards(): send_values = jnp.zeros((tile_count, halves, slots, half_bins), jnp.float...  26 us
    dot_general x4, matrix products, transpose_product(): lax.dot_general(matrix, values, (((0,), (0,)), ((), ())), preferred_eleme...  19.7 us
    scatter x2, local copies, waits for them, and re-layouts, shards(): send_cells = jnp.full((tile_count, halves, slots), -1, jnp.int32).at[poin...  13.3 us
    mul x4, other arithmetic, upwind(): face_flux = courant * face_value  12.8 us
    ppermute x2, starting transfers between devices, with_halo(): lax.ppermute(lax.slice_in_dim(block, 0, width, axis=dim), axis, backward)  12.7 us
  transfers between devices with their start and end apart: 6, of which 5 were waited for; matrix products, arithmetic and copies ran while one was open for 23% of the time, Pallas kernels for 0%

commit v1 on v0

v1 whole, which is shorter than its diff:
```python
import functools
import math

import jax
import jax.numpy as jnp
import numpy as np
from jax import lax
from jax.experimental import pallas as pl
from jax.experimental.pallas import tpu as pltpu
from jax.sharding import PartitionSpec as P

NTH = 36
STEPS = 2
LANES = 128
ROWS = 256

LAMBDA = 0.25
COEF_THREE = (1.0 + LAMBDA) ** (-4)
COEF_FOUR = (1.0 - LAMBDA) ** (-4)
COEF_BOTH = (1.0 - LAMBDA * LAMBDA) ** (-4)
CFL_LIMIT = 0.8
WIND_RATE = 0.2


def round_up(value, step):
    return -(-value // step) * step


def bin_tables(count_bins):
    bin_range = np.arange(count_bins)
    theta = 2.0 * math.pi * (bin_range % NTH) / NTH
    group_speed = CFL_LIMIT * 1.1 ** (-(bin_range // NTH).astype(np.float64))
    return np.cos(theta), np.sin(theta), group_speed


def stencil(courant):
    bend = (1.0 - courant * courant) / 6.0
    up = courant >= 0.0
    zero = np.zeros_like(courant)
    left = courant * np.where(up, -bend, zero)
    here = courant * (0.5 + 0.5 * courant + np.where(up, 2.0 * bend, -bend))
    right = courant * (0.5 - 0.5 * courant + np.where(up, -bend, 2.0 * bend))
    far = courant * np.where(up, zero, -bend)
    return np.stack([left, here - left, 1.0 + right - here, far - right, -far])


def source_kernel(owners, per, spectra, wind, index, weight, nl_coef, tables, out,
                  index_pad, weight_pad, nl_pad, flat_t, low_t, wind_t, matrix, inter, total):
    count_bins, points = spectra.shape
    padded = flat_t.shape[1]
    chunks = padded // LANES
    whole = count_bins // LANES
    rest = count_bins - whole * LANES
    index_pad[...] = jnp.full(index_pad.shape, -1, jnp.int32)
    index_pad[:, :count_bins] = index[...]
    weight_pad[...] = jnp.zeros(weight_pad.shape, jnp.float32)
    weight_pad[:, :count_bins] = weight[...].astype(jnp.float32)
    nl_pad[...] = jnp.zeros(nl_pad.shape, jnp.float32)
    nl_pad[:, :count_bins] = nl_coef[...]
    for half in range(points // LANES):
        span = slice(half * LANES, (half + 1) * LANES)
        for block in range(chunks):
            if block < whole:
                values = spectra[block * LANES:(block + 1) * LANES, span]
            else:
                values = jnp.concatenate(
                    [spectra[whole * LANES:, span], jnp.zeros((LANES - rest, LANES), jnp.float32)], axis=0
                )
            turned = values.T
            flat_t[span, block * LANES:(block + 1) * LANES] = turned
            low_t[span, block * LANES:(block + 1) * LANES] = turned.astype(jnp.bfloat16)
        drive = jnp.concatenate([wind[:, span], jnp.zeros((LANES - 2, LANES), jnp.float32)], axis=0)
        wind_t[span, :] = drive.T

    def chunk_step(chunk, carry):
        lane = pl.multiple_of(chunk * LANES, LANES)
        lanes = pl.ds(lane, LANES)
        wide = pl.multiple_of(chunk * 4 * LANES, 4 * LANES)
        rows_index = [index_pad[pl.ds(r, 1), lanes] for r in range(16)]
        rows_weight = [weight_pad[pl.ds(r, 1), lanes] for r in range(16)]
        members = [jnp.zeros((points, 2 * LANES), jnp.float32) for _ in range(2)]
        for start in range(0, padded, ROWS):
            size = min(ROWS, padded - start)
            place = lax.broadcasted_iota(jnp.int32, (size, LANES), 0) + start
            for mirror in range(2):
                for member in range(2):
                    block = jnp.zeros((size, LANES), jnp.float32)
                    for corner in range(4):
                        r = mirror * 8 + member * 4 + corner
                        block = jnp.where(place == rows_index[r], rows_weight[r], block)
                    matrix[start:start + size, pl.ds(wide + (mirror * 2 + member) * LANES, LANES)] = (
                        block.astype(jnp.bfloat16)
                    )
                members[mirror] = members[mirror] + jnp.dot(
                    low_t[:, start:start + size],
                    matrix[start:start + size, pl.ds(wide + mirror * 2 * LANES, 2 * LANES)],
                    preferred_element_type=jnp.float32,
                )
        values = flat_t[:, lanes]
        coef = nl_pad[:, lanes]
        drive = jnp.maximum(
            wind_t[:, 0:1] * tables[0:1, lanes] + wind_t[:, 1:2] * tables[1:2, lanes], 0.0
        )
        base = values + WIND_RATE * drive * values
        for mirror in range(2):
            third = members[mirror][:, :LANES]
            fourth = members[mirror][:, LANES:]
            interaction = coef * (
                values * values * (COEF_THREE * third + COEF_FOUR * fourth)
                - 2.0 * COEF_BOTH * values * third * fourth
            )
            base = base - 2.0 * interaction
            for half in range(points // LANES):
                span = slice(half * LANES, (half + 1) * LANES)
                turned = interaction[span].T.astype(jnp.bfloat16)
                for member in range(2):
                    inter[pl.ds(wide + (mirror * 2 + member) * LANES, LANES), span] = turned
        for half in range(points // LANES):
            span = slice(half * LANES, (half + 1) * LANES)
            total[lanes, span] = base[span].T
        return carry

    lax.fori_loop(0, chunks, chunk_step, 0)
    for start in range(0, padded, ROWS):
        size = min(ROWS, padded - start)
        total[start:start + size, :] += jnp.dot(
            matrix[start:start + size, :], inter[...], preferred_element_type=jnp.float32
        )
    tiles, halves = owners
    half_bins = count_bins // halves
    for tile in range(tiles):
        for side in range(halves):
            first = side * half_bins + tile * per
            valid = min(per, half_bins - tile * per)
            if valid <= 0:
                continue
            for half in range(points // LANES):
                out[tile * halves + side, half * per:half * per + valid, :] = total[
                    first:first + valid, half * LANES:(half + 1) * LANES
                ]


def source_terms(owners, per, spectra, wind, index, weight, nl_coef):
    count_bins, points = spectra.shape
    padded = round_up(count_bins, LANES)
    cosine, sine, _ = bin_tables(count_bins)
    tables = np.zeros((2, padded), np.float32)
    tables[0, :count_bins] = cosine
    tables[1, :count_bins] = sine
    group = owners[0] * owners[1]
    rows = per * (points // LANES)
    return pl.pallas_call(
        functools.partial(source_kernel, owners, per),
        out_shape=jax.ShapeDtypeStruct((group, rows, LANES), jnp.float32),
        scratch_shapes=[
            pltpu.VMEM((16, padded), jnp.int32),
            pltpu.VMEM((16, padded), jnp.float32),
            pltpu.VMEM((1, padded), jnp.float32),
            pltpu.VMEM((points, padded), jnp.float32),
            pltpu.VMEM((points, padded), jnp.bfloat16),
            pltpu.VMEM((points, LANES), jnp.float32),
            pltpu.VMEM((padded, 4 * padded), jnp.bfloat16),
            pltpu.VMEM((4 * padded, points), jnp.bfloat16),
            pltpu.VMEM((padded, points), jnp.float32),
        ],
        compiler_params=pltpu.CompilerParams(vmem_limit_bytes=52 * 1024 * 1024),
        name="source_terms",
    )(spectra, wind, index, weight, nl_coef, jnp.asarray(tables))


def propagate_kernel(per, columns_tile, base, got, rel, taps, out, ranked, split, first, second):
    group = got.shape[0]
    columns = rel.shape[0]
    halves = got.shape[1] // per
    padded = first.shape[1]
    split_rows = split.shape[0] // 2
    fill = jnp.zeros((LANES - per, LANES), jnp.float32) if per < LANES else None

    def order(owner, carry):
        for half in range(halves):
            values = got[owner, half * per:(half + 1) * per, :]
            if fill is not None:
                values = jnp.concatenate([values, fill], axis=0)
            ranked[pl.ds(half * LANES * group + owner, LANES, stride=group), :] = values.T
        return carry

    lax.fori_loop(0, group, order, 0)

    rank_tiles = ranked.shape[0] // LANES

    def halve(tile, carry):
        start = pl.multiple_of(tile * LANES, LANES)
        turned = ranked[pl.ds(start, LANES), :].T[:split_rows]
        high = turned.astype(jnp.bfloat16)
        split[:split_rows, pl.ds(start, LANES)] = high
        split[split_rows:, pl.ds(start, LANES)] = (turned - high.astype(jnp.float32)).astype(jnp.bfloat16)
        return carry

    lax.fori_loop(0, rank_tiles, halve, 0)
    split[:, rank_tiles * LANES:] = jnp.zeros((2 * split_rows, LANES), jnp.bfloat16)

    place = lax.broadcasted_iota(jnp.int32, (2 * LANES, LANES), 0)

    def expand(column, carry):
        start = pl.multiple_of(base[column], LANES)
        onehot = jnp.where(place == rel[pl.ds(column, 1), :], 1.0, 0.0).astype(jnp.bfloat16)
        both = jnp.dot(split[:, pl.ds(start, 2 * LANES)], onehot, preferred_element_type=jnp.float32)
        first[column] = both[:padded] + both[split_rows:split_rows + padded]
        return carry

    lax.fori_loop(0, columns, expand, 0)

    lane = lax.broadcasted_iota(jnp.int32, (8, LANES), 1)
    for tile in range(padded // 8):
        span = slice(tile * 8, (tile + 1) * 8)
        x_taps = [jnp.broadcast_to(taps[span, k:k + 1], (8, LANES)) for k in range(5)]
        y_taps = []
        for k in range(5):
            tap = jnp.broadcast_to(taps[span, 5 + k:6 + k], (8, LANES))
            shift = k - 2
            inside = (lane + shift >= 0) & (lane + shift < LANES)
            y_taps.append(jnp.where(inside, tap, 0.0))
        valid = min(8, per - tile * 8)

        def sweep(source, target, column):
            value = x_taps[2] * source[column, span, :]
            for k in (0, 1, 3, 4):
                if isinstance(column, int):
                    other = (column + k - 2) % columns
                else:
                    other = column + (k - 2)
                    other = jnp.where(other < 0, other + columns, other)
                    other = jnp.where(other >= columns, other - columns, other)
                value = value + x_taps[k] * source[other, span, :]
            sea = jnp.where(rel[pl.ds(column, 1), :] >= 0, 1.0, 0.0)
            value = value * sea
            moved = y_taps[2] * value
            for k in (0, 1, 3, 4):
                moved = moved + y_taps[k] * pltpu.roll(value, (2 - k) % LANES, 1)
            return moved * sea

        def one(column, carry):
            second[column, span, :] = sweep(first, second, column)
            return carry

        lax.fori_loop(0, columns, one, 0, unroll=8)

        def two(column, carry):
            result = sweep(second, None, column)
            owner = column // columns_tile
            start = (owner * per + tile * 8) * columns_tile + column % columns_tile
            if valid == 8:
                out[pl.ds(start, 8, stride=columns_tile), :] = result
            else:
                for row in range(valid):
                    out[pl.ds(start + row * columns_tile, 1), :] = result[row:row + 1]
            return carry

        lax.fori_loop(0, columns, two, 0, unroll=8)


def propagate(per, columns_tile, base, got, rel, taps):
    group, rows, _ = got.shape
    columns = rel.shape[0]
    points = rows // per * LANES
    padded = round_up(per, 8)
    split_rows = round_up(per, 16)
    smem = pl.BlockSpec(memory_space=pltpu.SMEM)
    vmem = pl.BlockSpec(memory_space=pltpu.VMEM)
    return pl.pallas_call(
        functools.partial(propagate_kernel, per, columns_tile),
        out_shape=jax.ShapeDtypeStruct((columns * per, LANES), jnp.float32),
        in_specs=[smem, vmem, vmem, vmem],
        out_specs=vmem,
        scratch_shapes=[
            pltpu.VMEM((group * points, LANES), jnp.float32),
            pltpu.VMEM((2 * split_rows, group * points + LANES), jnp.bfloat16),
            pltpu.VMEM((columns, padded, LANES), jnp.float32),
            pltpu.VMEM((columns, padded, LANES), jnp.float32),
        ],
        compiler_params=pltpu.CompilerParams(vmem_limit_bytes=52 * 1024 * 1024),
        name="propagate",
    )(base, got, rel, taps)


def shards(spectra, wind, mask, dia_index, dia_weight, nl_coef):
    count_bins = spectra.shape[0]
    tiles = lax.axis_size("tile")
    halves = lax.axis_size("bin")
    columns, latitudes = mask.shape
    columns_tile = columns // tiles
    half_bins = count_bins // halves
    per = -(-half_bins // tiles)
    padded = round_up(per, 8)

    payload = source_terms(
        (tiles, halves), per, spectra, wind, dia_index.reshape(16, count_bins),
        dia_weight.reshape(16, count_bins), nl_coef.reshape(1, count_bins),
    )
    got = lax.all_to_all(payload, ("tile", "bin"), split_axis=0, concat_axis=0, tiled=True)

    cosine, sine, speed = bin_tables(count_bins)
    weights = np.concatenate([stencil(speed * cosine), stencil(speed * sine)])
    table = np.zeros((halves, tiles, padded, LANES), np.float32)
    for side in range(halves):
        for tile in range(tiles):
            valid = max(0, min(per, half_bins - tile * per))
            begin = side * half_bins + tile * per
            table[side, tile, :valid, :10] = weights[:, begin:begin + valid].T
    taps = lax.dynamic_slice(
        jnp.asarray(table),
        (lax.axis_index("bin"), lax.axis_index("tile"), 0, 0),
        (1, 1, padded, LANES),
    ).reshape(padded, LANES)

    ones = mask.astype(jnp.bfloat16)
    upto = jnp.dot(ones, jnp.asarray(np.triu(np.ones((latitudes, latitudes))), jnp.bfloat16),
                   preferred_element_type=jnp.float32)
    before = jnp.dot(jnp.asarray(np.tril(np.ones((columns, columns)), -1), jnp.bfloat16), ones,
                     preferred_element_type=jnp.float32).sum(axis=1).astype(jnp.int32)
    total = payload.shape[0] * spectra.shape[1]
    base = jnp.minimum(before // LANES * LANES, total - LANES)
    rel = jnp.where(mask == 1, upto.astype(jnp.int32) - 1 + (before - base)[:, None], -1)

    moved = propagate(per, columns_tile, base, got, rel, taps)
    result = lax.all_to_all(
        moved.reshape(tiles, per, columns_tile, latitudes), "tile", split_axis=0, concat_axis=0, tiled=True
    ).reshape(tiles * per, columns_tile, latitudes)
    return result[:half_bins]


def solution(mesh):
    in_specs = (
        P(None, ("band", "tile", "bin")),
        P(None, ("band", "tile", "bin")),
        P(None, "band"),
        P(),
        P(),
        P(),
    )
    out_specs = P("bin", "tile", "band")
    return jax.shard_map(shards, mesh=mesh, in_specs=in_specs, out_specs=out_specs, check_vma=False)
```

time: 300 us -> 187 us (0.62); the launches traced: 296 us -> 186 us
  local copies, waits for them, and re-layouts: 96.8 us -> 7.45 us
  waiting for transfers between devices: 104 us -> 27.4 us
  Pallas kernels: 0 us -> 74.2 us
  blocking collectives: 0 us -> 69.5 us
  matrix products: 36.6 us -> 0.3 us
  other arithmetic: 27.3 us -> 0.02 us
  starting transfers between devices: 30.6 us -> 7.39 us
    scatter x6 -> x0, local copies, waits for them, and re-layouts: 76.4 us -> none  [the longest x1 30.4 us: shards(): cell_of = jnp.zeros((points,), jnp.int32).at[targets].set(jnp.arange(flat...]
    pallas_call x0 -> x2, Pallas kernels: none -> 74.2 us  [the longest x1 48.4 us: propagate(): pl.pallas_call(functools.partial(propagate_kernel, per, columns_tile), ou...]
    all_to_all x0 -> x1, blocking collectives: none -> 69.5 us  [shards(): lax.all_to_all(moved.reshape(tiles, per, columns_tile, latitudes), 'tile'...]
    ppermute x4 -> x0, waiting for transfers between devices: 53.4 us -> none  [the longest x2 43.4 us: with_halo(): lax.ppermute(lax.slice_in_dim(block, block.shape[dim] - width, None, axis...]
    dot_general x8 -> x2, matrix products: 36.6 us -> 0.3 us  [the longest x1 0.23 us: shards(): jnp.dot(jnp.asarray(np.tril(np.ones((columns, columns)), -1), jnp.bfloat1...]
    all_to_all x2 -> x1, waiting for transfers between devices: 50.7 us -> 27.4 us  [shards(): lax.all_to_all(payload, ('tile', 'bin'), split_axis=0, concat_axis=0, til...]
    ppermute x4 -> x0, starting transfers between devices: 17 us -> none  [the longest x2 12.7 us: with_halo(): lax.ppermute(lax.slice_in_dim(block, 0, width, axis=dim), axis, backward)]
    mul x11 -> x0, other arithmetic: 15.2 us -> none  [the longest x4 12.8 us: upwind(): face_flux = courant * face_value]
  transfers between devices with their start and end apart: 6 -> 1, of which waited for: 5 -> 1; matrix products, arithmetic and copies ran while one was open for 23% -> 1% of each run, Pallas kernels for 0% -> 0%
where the time goes in v1:
time: 187 us; the launch traced here: 186 us
  Pallas kernels  74.2 us (40%)
  blocking collectives  69.5 us (37%)
  waiting for transfers between devices  27.4 us (15%)
  local copies, waits for them, and re-layouts  7.45 us (4%)
  starting transfers between devices  7.39 us (4%)
    all_to_all x1, blocking collectives, shards(): lax.all_to_all(moved.reshape(tiles, per, columns_tile, latitudes), 'tile'...  69.5 us
    pallas_call x1, Pallas kernels, propagate(): pl.pallas_call(functools.partial(propagate_kernel, per, columns_tile), ou...  48.4 us
    all_to_all x1, waiting for transfers between devices, shards(): lax.all_to_all(payload, ('tile', 'bin'), split_axis=0, concat_axis=0, til...  27.4 us
    pallas_call x1, Pallas kernels, source_terms(): pl.pallas_call(functools.partial(source_kernel, owners, per), out_shape=j...  25.8 us
    all_to_all x1, starting transfers between devices, shards(): lax.all_to_all(payload, ('tile', 'bin'), split_axis=0, concat_axis=0, til...  7.39 us
    unnamed x13, local copies, waits for them, and re-layouts  4.22 us
  transfers between devices with their start and end apart: 1, of which 1 were waited for; matrix products, arithmetic and copies ran while one was open for 1% of the time, Pallas kernels for 0%

profile of v1, /device:TPU:0, one launch (start us, length us, event | category | flops | bytes accessed | tf_op | source)
XLA Modules:
  0.0 186.4 jit_solution(58497838320611550)
XLA Ops:
  0.0 0.7 reshape.41.nl_coef
  0.7 0.8 reshape.40.weight
  1.5 0.9 reshape.39.index
  2.4 0.0 copy-start
  2.5 1.3 copy-done
  3.8 0.0 copy-start.1
  3.8 0.7 copy-done.1
  4.5 0.0 copy-start.2
  4.5 0.7 copy-done.2
  5.2 0.0 copy-start.3
  5.2 0.0 copy-start.5
  5.2 0.0 copy-start.4
  5.2 25.8 %source_terms.1 = f32[16,162,128]{2,1,0:T(8,128)} custom-call(f32[1296,256]{1,0:T(8,128)S(1)} %copy-done, f32[2,256]{1,0:T(2,128)S(1)} %copy-done.2, s32[16,1296]{1,0:T(8,128)S(1)} %reshape.39.index, bf16[16,1296]{1,0:T(8,128)(2,1)S(1)} %reshape.40.weight, f32[1,1296]{1,0:T(1,128)S(1)} %reshape.41.nl_coef, f32[2,1408]{1,0:T(2,128)S(1)} %copy-done.1), custom_call_target="tpu_custom_call" | custom-call | tf_op jit(solution)/shard_map/source_terms/pallas_call | solution.py:152
  31.0 7.4 %all-to-all-start = ((f32[16,162,128]{2,1,0:T(8,128)}), f32[16,162,128]{2,1,0:T(8,128)S(1)}, u32[]{:S(2)}, u32[]{:S(2)}) async-start(f32[16,162,128]{2,1,0:T(8,128)} %source_terms.1), calls=%async_computation | async-start | bytes 2752512 | tf_op jit(solution)/shard_map/all_to_all | solution.py:300
  38.4 0.8 dynamic-slice_bitcast_fusion.taps
  39.2 0.0 copy-done.3
  39.2 0.0 copy-done.5
  39.2 0.2 convolution_reduce_fusion
  39.5 0.0 copy-done.4
  39.5 0.1 fusion.3.rel
  39.6 27.4 %all-to-all-done.got = f32[16,162,128]{2,1,0:T(8,128)S(1)} async-done(((f32[16,162,128]{2,1,0:T(8,128)}), f32[16,162,128]{2,1,0:T(8,128)S(1)}, u32[]{:S(2)}, u32[]{:S(2)}) %all-to-all-start) | async-done | bytes 1327136 | tf_op jit(solution)/shard_map/all_to_all | solution.py:300
  67.0 48.4 %propagate.1 = f32[5184,128]{1,0:T(8,128)} custom-call(s32[64]{0:T(128)S(1)} %get-tuple-element.6.base, f32[16,162,128]{2,1,0:T(8,128)S(1)} %all-to-all-done.got, s32[64,128]{1,0:T(8,128)S(1)} %fusion.3.rel, f32[88,128]{1,0:T(8,128)S(1)} %dynamic-slice_bitcast_fusion.taps), custom_call_target="tpu_custom_call" | custom-call | tf_op jit(solution)/shard_map/propagate/pallas_call | solution.py:270
  115.4 69.5 %all_to_all.10 = f32[8,81,8,128]{3,2,1,0:T(8,128)S(1)} all-to-all(f32[8,81,8,128]{3,2,1,0:T(8,128)} %bitcast.10), channel_id=1, replica_groups=mesh['band'=2,'tile'=8,'bin'=2] {'tile'}, dimensions={0} | all-to-all | bytes 5308416 | tf_op jit(solution)/shard_map/all_to_all | solution.py:326
  184.9 1.5 copy.12
  (1 shorter events, 0.0 us)
Async XLA Ops:
  2.4 1.3 copy-start
  3.8 0.7 copy-start.1
  4.5 0.7 copy-start.2
  5.2 34.1 %copy-start.3 = (s32[64,128]{1,0:T(8,128)S(1)}, s32[64,128]{1,0:T(8,128)}, u32[]{:S(2)}) copy-start(s32[64,128]{1,0:T(8,128)} %param.12) | copy-start | bytes 98308
  5.2 34.1 %copy-start.5 = (bf16[64,64]{1,0:T(8,128)(2,1)S(1)}, bf16[64,64]{1,0:T(8,128)(2,1)}, u32[]{:S(2)}) copy-start(bf16[64,64]{1,0:T(8,128)(2,1)} %constant.49.clone) | copy-start | bytes 24580
  5.2 34.3 %copy-start.4 = (bf16[128,128]{1,0:T(8,128)(2,1)S(1)}, bf16[128,128]{1,0:T(8,128)(2,1)}, u32[]{:S(2)}) copy-start(bf16[128,128]{1,0:T(8,128)(2,1)} %constant.48.clone) | copy-start | bytes 98308
  31.0 36.0 %all-to-all-start = ((f32[16,162,128]{2,1,0:T(8,128)}), f32[16,162,128]{2,1,0:T(8,128)S(1)}, u32[]{:S(2)}, u32[]{:S(2)}) async-start(f32[16,162,128]{2,1,0:T(8,128)} %source_terms.1), calls=%async_computation | async-start | bytes 2752512 | tf_op jit(solution)/shard_map/all_to_all | solution.py:300

commit v2 on v1

--- a/solution.py
+++ b/solution.py
@@ -168,115 +168,108 @@
     )(spectra, wind, index, weight, nl_coef, jnp.asarray(tables))
 
 
-def propagate_kernel(per, columns_tile, base, got, rel, taps, out, ranked, split, first, second):
+def propagate_kernel(per, columns_tile, halo, base, got, rel, taps, out, ranked, lined, middle, pick, sea):
     group = got.shape[0]
     columns = rel.shape[0]
     halves = got.shape[1] // per
-    padded = first.shape[1]
-    split_rows = split.shape[0] // 2
-    fill = jnp.zeros((LANES - per, LANES), jnp.float32) if per < LANES else None
+    fill = jnp.zeros((LANES - per, LANES), jnp.float32)
 
     def order(owner, carry):
         for half in range(halves):
-            values = got[owner, half * per:(half + 1) * per, :]
-            if fill is not None:
-                values = jnp.concatenate([values, fill], axis=0)
+            values = jnp.concatenate([got[owner, half * per:(half + 1) * per, :], fill], axis=0)
             ranked[pl.ds(half * LANES * group + owner, LANES, stride=group), :] = values.T
         return carry
 
-    lax.fori_loop(0, group, order, 0)
+    lax.fori_loop(0, group, order, 0, unroll=4)
 
     rank_tiles = ranked.shape[0] // LANES
-
-    def halve(tile, carry):
+    padded = lined.shape[0]
+
+    def line_up(tile, carry):
         start = pl.multiple_of(tile * LANES, LANES)
-        turned = ranked[pl.ds(start, LANES), :].T[:split_rows]
-        high = turned.astype(jnp.bfloat16)
-        split[:split_rows, pl.ds(start, LANES)] = high
-        split[split_rows:, pl.ds(start, LANES)] = (turned - high.astype(jnp.float32)).astype(jnp.bfloat16)
+        lined[:, pl.ds(start, LANES)] = ranked[pl.ds(start, LANES), :].T[:padded]
         return carry
 
-    lax.fori_loop(0, rank_tiles, halve, 0)
-    split[:, rank_tiles * LANES:] = jnp.zeros((2 * split_rows, LANES), jnp.bfloat16)
-
-    place = lax.broadcasted_iota(jnp.int32, (2 * LANES, LANES), 0)
-
-    def expand(column, carry):
-        start = pl.multiple_of(base[column], LANES)
-        onehot = jnp.where(place == rel[pl.ds(column, 1), :], 1.0, 0.0).astype(jnp.bfloat16)
-        both = jnp.dot(split[:, pl.ds(start, 2 * LANES)], onehot, preferred_element_type=jnp.float32)
-        first[column] = both[:padded] + both[split_rows:split_rows + padded]
-        return carry
-
-    lax.fori_loop(0, columns, expand, 0)
+    lax.fori_loop(0, rank_tiles, line_up, 0, unroll=4)
+    lined[:, rank_tiles * LANES:] = jnp.zeros((padded, LANES), jnp.float32)
+
+    for column in range(columns):
+        row = jnp.broadcast_to(rel[column:column + 1, :], (8, LANES))
+        pick[column] = row
+        sea[column] = jnp.where(row >= 0, 1.0, 0.0)
 
     lane = lax.broadcasted_iota(jnp.int32, (8, LANES), 1)
-    for tile in range(padded // 8):
-        span = slice(tile * 8, (tile + 1) * 8)
+
+    def bins_step(first_bin, valid):
+        span = pl.ds(first_bin, 8)
         x_taps = [jnp.broadcast_to(taps[span, k:k + 1], (8, LANES)) for k in range(5)]
         y_taps = []
         for k in range(5):
             tap = jnp.broadcast_to(taps[span, 5 + k:6 + k], (8, LANES))
-            shift = k - 2
-            inside = (lane + shift >= 0) & (lane + shift < LANES)
+            inside = (lane + (k - 2) >= 0) & (lane + (k - 2) < LANES)
             y_taps.append(jnp.where(inside, tap, 0.0))
-        valid = min(8, per - tile * 8)
-
-        def sweep(source, target, column):
-            value = x_taps[2] * source[column, span, :]
+
+        def expanded(column):
+            start = pl.multiple_of(base[column], LANES)
+            chosen = pick[column]
+            within = chosen & (LANES - 1)
+            low = jnp.take_along_axis(lined[span, pl.ds(start, LANES)], within, axis=1)
+            high = jnp.take_along_axis(lined[span, pl.ds(start + LANES, LANES)], within, axis=1)
+            return jnp.where(chosen >= LANES, high, low) * sea[column]
+
+        def sweep(values, column):
+            value = x_taps[2] * values[2]
             for k in (0, 1, 3, 4):
-                if isinstance(column, int):
-                    other = (column + k - 2) % columns
-                else:
-                    other = column + (k - 2)
-                    other = jnp.where(other < 0, other + columns, other)
-                    other = jnp.where(other >= columns, other - columns, other)
-                value = value + x_taps[k] * source[other, span, :]
-            sea = jnp.where(rel[pl.ds(column, 1), :] >= 0, 1.0, 0.0)
-            value = value * sea
+                value = value + x_taps[k] * values[k]
+            value = value * sea[column]
             moved = y_taps[2] * value
             for k in (0, 1, 3, 4):
                 moved = moved + y_taps[k] * pltpu.roll(value, (2 - k) % LANES, 1)
-            return moved * sea
-
-        def one(column, carry):
-            second[column, span, :] = sweep(first, second, column)
-            return carry
-
-        lax.fori_loop(0, columns, one, 0, unroll=8)
-
-        def two(column, carry):
-            result = sweep(second, None, column)
-            owner = column // columns_tile
-            start = (owner * per + tile * 8) * columns_tile + column % columns_tile
+            return moved * sea[column]
+
+        reach = halo // STEPS
+        first = {}
+        for column in range(columns):
+            first[column] = expanded(column)
+        for column in range(reach, columns - reach):
+            middle[column] = sweep([first[(column + k) % columns] for k in range(-2, 3)], column)
+        for column in range(halo, columns - halo):
+            result = sweep([middle[(column + k) % columns] for k in range(-2, 3)], column)
+            owner, place = divmod(column - halo, columns_tile)
+            start = (owner * per + first_bin) * columns_tile + place
             if valid == 8:
                 out[pl.ds(start, 8, stride=columns_tile), :] = result
             else:
                 for row in range(valid):
                     out[pl.ds(start + row * columns_tile, 1), :] = result[row:row + 1]
-            return carry
-
-        lax.fori_loop(0, columns, two, 0, unroll=8)
-
-
-def propagate(per, columns_tile, base, got, rel, taps):
+
+    def full_step(tile, carry):
+        bins_step(pl.multiple_of(tile * 8, 8), 8)
+        return carry
+
+    lax.fori_loop(0, per // 8, full_step, 0)
+    if per % 8:
+        bins_step(per // 8 * 8, per % 8)
+
+
+def propagate(per, columns_tile, halo, base, got, rel, taps):
     group, rows, _ = got.shape
     columns = rel.shape[0]
     points = rows // per * LANES
     padded = round_up(per, 8)
-    split_rows = round_up(per, 16)
     smem = pl.BlockSpec(memory_space=pltpu.SMEM)
     vmem = pl.BlockSpec(memory_space=pltpu.VMEM)
     return pl.pallas_call(
-        functools.partial(propagate_kernel, per, columns_tile),
-        out_shape=jax.ShapeDtypeStruct((columns * per, LANES), jnp.float32),
+        functools.partial(propagate_kernel, per, columns_tile, halo),
+        out_shape=jax.ShapeDtypeStruct(((columns - 2 * halo) * per, LANES), jnp.float32),
         in_specs=[smem, vmem, vmem, vmem],
         out_specs=vmem,
         scratch_shapes=[
             pltpu.VMEM((group * points, LANES), jnp.float32),
-            pltpu.VMEM((2 * split_rows, group * points + LANES), jnp.bfloat16),
-            pltpu.VMEM((columns, padded, LANES), jnp.float32),
-            pltpu.VMEM((columns, padded, LANES), jnp.float32),
+            pltpu.VMEM((padded, group * points + LANES), jnp.float32),
+            pltpu.VMEM((columns, 8, LANES), jnp.float32),
+            pltpu.VMEM((columns, 8, LANES), jnp.int32),
+            pltpu.VMEM((columns, 8, LANES), jnp.float32),
         ],
         compiler_params=pltpu.CompilerParams(vmem_limit_bytes=52 * 1024 * 1024),
         name="propagate",
@@ -322,7 +315,7 @@
     base = jnp.minimum(before // LANES * LANES, total - LANES)
     rel = jnp.where(mask == 1, upto.astype(jnp.int32) - 1 + (before - base)[:, None], -1)
 
-    moved = propagate(per, columns_tile, base, got, rel, taps)
+    moved = propagate(per, columns_tile, 0, base, got, rel, taps)
     result = lax.all_to_all(
         moved.reshape(tiles, per, columns_tile, latitudes), "tile", split_axis=0, concat_axis=0, tiled=True
     ).reshape(tiles * per, columns_tile, latitudes)

time: 187 us -> 155 us (0.83)
  Pallas kernels: 74.2 us -> 42.2 us
    pallas_call x1, Pallas kernels: 48.4 us -> 16.4 us  [propagate(): pl.pallas_call(functools.partial(propagate_kernel, per, columns_tile, hal...]
where the time goes in v2:
time: 155 us; the launch traced here: 154 us
  blocking collectives  69.5 us (45%)
  Pallas kernels  42.2 us (27%)
  waiting for transfers between devices  27.4 us (18%)
  local copies, waits for them, and re-layouts  7.45 us (5%)
  starting transfers between devices  7.39 us (5%)
    all_to_all x1, blocking collectives, shards(): lax.all_to_all(moved.reshape(tiles, per, columns_tile, latitudes), 'tile'...  69.5 us
    all_to_all x1, waiting for transfers between devices, shards(): lax.all_to_all(payload, ('tile', 'bin'), split_axis=0, concat_axis=0, til...  27.4 us
    pallas_call x1, Pallas kernels, source_terms(): pl.pallas_call(functools.partial(source_kernel, owners, per), out_shape=j...  25.8 us
    pallas_call x1, Pallas kernels, propagate(): pl.pallas_call(functools.partial(propagate_kernel, per, columns_tile, hal...  16.4 us
    all_to_all x1, starting transfers between devices, shards(): lax.all_to_all(payload, ('tile', 'bin'), split_axis=0, concat_axis=0, til...  7.39 us
    unnamed x13, local copies, waits for them, and re-layouts  4.22 us
  transfers between devices with their start and end apart: 1, of which 1 were waited for; matrix products, arithmetic and copies ran while one was open for 1% of the time, Pallas kernels for 0%

profile of v2, /device:TPU:0, one launch (start us, length us, event | category | flops | bytes accessed | tf_op | source)
XLA Modules:
  0.0 154.4 jit_solution(6099063796614455253)
XLA Ops:
  0.0 0.7 reshape.41.nl_coef
  0.7 0.8 reshape.40.weight
  1.5 0.9 reshape.39.index
  2.4 0.0 copy-start
  2.5 1.3 copy-done
  3.8 0.0 copy-start.1
  3.8 0.7 copy-done.1
  4.5 0.0 copy-start.2
  4.5 0.7 copy-done.2
  5.2 0.0 copy-start.3
  5.2 0.0 copy-start.5
  5.2 0.0 copy-start.4
  5.2 25.8 %source_terms.1 = f32[16,162,128]{2,1,0:T(8,128)} custom-call(f32[1296,256]{1,0:T(8,128)S(1)} %copy-done, f32[2,256]{1,0:T(2,128)S(1)} %copy-done.2, s32[16,1296]{1,0:T(8,128)S(1)} %reshape.39.index, bf16[16,1296]{1,0:T(8,128)(2,1)S(1)} %reshape.40.weight, f32[1,1296]{1,0:T(1,128)S(1)} %reshape.41.nl_coef, f32[2,1408]{1,0:T(2,128)S(1)} %copy-done.1), custom_call_target="tpu_custom_call" | custom-call | tf_op jit(solution)/shard_map/source_terms/pallas_call | solution.py:152
  31.0 7.4 %all-to-all-start = ((f32[16,162,128]{2,1,0:T(8,128)}), f32[16,162,128]{2,1,0:T(8,128)S(1)}, u32[]{:S(2)}, u32[]{:S(2)}) async-start(f32[16,162,128]{2,1,0:T(8,128)} %source_terms.1), calls=%async_computation | async-start | bytes 2752512 | tf_op jit(solution)/shard_map/all_to_all | solution.py:293
  38.4 0.8 dynamic-slice_bitcast_fusion.taps
  39.2 0.0 copy-done.3
  39.2 0.0 copy-done.5
  39.2 0.2 convolution_reduce_fusion
  39.5 0.0 copy-done.4
  39.5 0.1 fusion.3.rel
  39.6 27.4 %all-to-all-done.got = f32[16,162,128]{2,1,0:T(8,128)S(1)} async-done(((f32[16,162,128]{2,1,0:T(8,128)}), f32[16,162,128]{2,1,0:T(8,128)S(1)}, u32[]{:S(2)}, u32[]{:S(2)}) %all-to-all-start) | async-done | bytes 1327136 | tf_op jit(solution)/shard_map/all_to_all | solution.py:293
  67.0 16.4 %propagate.1 = f32[5184,128]{1,0:T(8,128)} custom-call(s32[64]{0:T(128)S(1)} %get-tuple-element.6.base, f32[16,162,128]{2,1,0:T(8,128)S(1)} %all-to-all-done.got, s32[64,128]{1,0:T(8,128)S(1)} %fusion.3.rel, f32[88,128]{1,0:T(8,128)S(1)} %dynamic-slice_bitcast_fusion.taps), custom_call_target="tpu_custom_call" | custom-call | tf_op jit(solution)/shard_map/propagate/pallas_call | solution.py:262
  83.3 69.5 %all_to_all.10 = f32[8,81,8,128]{3,2,1,0:T(8,128)S(1)} all-to-all(f32[8,81,8,128]{3,2,1,0:T(8,128)} %bitcast.10), channel_id=1, replica_groups=mesh['band'=2,'tile'=8,'bin'=2] {'tile'}, dimensions={0} | all-to-all | bytes 5308416 | tf_op jit(solution)/shard_map/all_to_all | solution.py:319
  152.9 1.5 copy.12
  (1 shorter events, 0.0 us)
Async XLA Ops:
  2.4 1.3 copy-start
  3.8 0.7 copy-start.1
  4.5 0.7 copy-start.2
  5.2 34.1 %copy-start.3 = (s32[64,128]{1,0:T(8,128)S(1)}, s32[64,128]{1,0:T(8,128)}, u32[]{:S(2)}) copy-start(s32[64,128]{1,0:T(8,128)} %param.12) | copy-start | bytes 98308
  5.2 34.1 %copy-start.5 = (bf16[64,64]{1,0:T(8,128)(2,1)S(1)}, bf16[64,64]{1,0:T(8,128)(2,1)}, u32[]{:S(2)}) copy-start(bf16[64,64]{1,0:T(8,128)(2,1)} %constant.49.clone) | copy-start | bytes 24580
  5.2 34.3 %copy-start.4 = (bf16[128,128]{1,0:T(8,128)(2,1)S(1)}, bf16[128,128]{1,0:T(8,128)(2,1)}, u32[]{:S(2)}) copy-start(bf16[128,128]{1,0:T(8,128)(2,1)} %constant.48.clone) | copy-start | bytes 98308
  31.0 36.0 %all-to-all-start = ((f32[16,162,128]{2,1,0:T(8,128)}), f32[16,162,128]{2,1,0:T(8,128)S(1)}, u32[]{:S(2)}, u32[]{:S(2)}) async-start(f32[16,162,128]{2,1,0:T(8,128)} %source_terms.1), calls=%async_computation | async-start | bytes 2752512 | tf_op jit(solution)/shard_map/all_to_all | solution.py:293

commit v3 on v2

--- a/solution.py
+++ b/solution.py
@@ -13,6 +13,7 @@
 STEPS = 2
 LANES = 128
 ROWS = 256
+RING = 40
 
 LAMBDA = 0.25
 COEF_THREE = (1.0 + LAMBDA) ** (-4)
@@ -45,57 +46,99 @@
 
 
 def source_kernel(owners, per, spectra, wind, index, weight, nl_coef, tables, out,
-                  index_pad, weight_pad, nl_pad, flat_t, low_t, wind_t, matrix, inter, total):
+                  code, weight_pad, nl_pad, spaced, flat_t, low_t, wind_t, matrix, inter, total):
     count_bins, points = spectra.shape
     padded = flat_t.shape[1]
     chunks = padded // LANES
+    rings = count_bins // NTH
+    depth = spaced.shape[0]
     whole = count_bins // LANES
     rest = count_bins - whole * LANES
-    index_pad[...] = jnp.full(index_pad.shape, -1, jnp.int32)
-    index_pad[:, :count_bins] = index[...]
+
+    code[...] = jnp.zeros(code.shape, jnp.int32)
     weight_pad[...] = jnp.zeros(weight_pad.shape, jnp.float32)
-    weight_pad[:, :count_bins] = weight[...].astype(jnp.float32)
     nl_pad[...] = jnp.zeros(nl_pad.shape, jnp.float32)
-    nl_pad[:, :count_bins] = nl_coef[...]
+    nl_pad[:, :count_bins] = nl_coef[...].reshape(1, count_bins)
+    for mirror in range(2):
+        for member in range(2):
+            row = (mirror * 2 + member) * 4
+            bins = index[mirror, member]
+            ring = ((bins.astype(jnp.float32) + 0.5) * (1.0 / NTH)).astype(jnp.int32)
+            lowest = jnp.minimum(jnp.minimum(ring[0:1], ring[1:2]), jnp.minimum(ring[2:3], ring[3:4]))
+            direction = bins - ring * NTH
+            code[row:row + 4, :count_bins] = jnp.where(ring == lowest, direction, direction + RING)
+            code[16 + mirror * 2 + member:17 + mirror * 2 + member, :count_bins] = lowest
+            weight_pad[row:row + 4, :count_bins] = weight[mirror, member].astype(jnp.float32)
+
+    gap = jnp.zeros((RING - NTH, points), jnp.float32)
+    for ring in range(rings):
+        spaced[ring * RING:ring * RING + NTH, :] = spectra[ring * NTH:(ring + 1) * NTH, :]
+        spaced[ring * RING + NTH:(ring + 1) * RING, :] = gap
+    spaced[rings * RING:, :] = jnp.zeros((depth - rings * RING, points), jnp.float32)
     for half in range(points // LANES):
         span = slice(half * LANES, (half + 1) * LANES)
+        for block in range(depth // LANES):
+            lanes = slice(block * LANES, (block + 1) * LANES)
+            low_t[span, lanes] = spaced[lanes, span].T.astype(jnp.bfloat16)
         for block in range(chunks):
+            lanes = slice(block * LANES, (block + 1) * LANES)
             if block < whole:
-                values = spectra[block * LANES:(block + 1) * LANES, span]
+                values = spectra[lanes, span]
             else:
                 values = jnp.concatenate(
                     [spectra[whole * LANES:, span], jnp.zeros((LANES - rest, LANES), jnp.float32)], axis=0
                 )
-            turned = values.T
-            flat_t[span, block * LANES:(block + 1) * LANES] = turned
-            low_t[span, block * LANES:(block + 1) * LANES] = turned.astype(jnp.bfloat16)
+            flat_t[span, lanes] = values.T
         drive = jnp.concatenate([wind[:, span], jnp.zeros((LANES - 2, LANES), jnp.float32)], axis=0)
         wind_t[span, :] = drive.T
+
+    used = rings * RING
+    matrix[used:, :] = jnp.zeros((depth - used, matrix.shape[1]), jnp.bfloat16)
 
     def chunk_step(chunk, carry):
         lane = pl.multiple_of(chunk * LANES, LANES)
         lanes = pl.ds(lane, LANES)
         wide = pl.multiple_of(chunk * 4 * LANES, 4 * LANES)
-        rows_index = [index_pad[pl.ds(r, 1), lanes] for r in range(16)]
-        rows_weight = [weight_pad[pl.ds(r, 1), lanes] for r in range(16)]
+        place = lax.broadcasted_iota(jnp.int32, (RING, LANES), 0)
+        nothing = jnp.zeros((RING, LANES), jnp.float32)
+        patterns = []
+        for pair in range(4):
+            low = nothing
+            high = nothing
+            for corner in range(4):
+                r = pair * 4 + corner
+                where = code[pl.ds(r, 1), lanes]
+                amount = jnp.broadcast_to(weight_pad[pl.ds(r, 1), lanes], (RING, LANES))
+                low = jnp.where(place == where, amount, low)
+                high = jnp.where(place + RING == where, amount, high)
+            lowest = jnp.broadcast_to(code[pl.ds(16 + pair, 1), lanes], (8, LANES))
+            patterns.append((low, high, lowest))
         members = [jnp.zeros((points, 2 * LANES), jnp.float32) for _ in range(2)]
-        for start in range(0, padded, ROWS):
-            size = min(ROWS, padded - start)
-            place = lax.broadcasted_iota(jnp.int32, (size, LANES), 0) + start
-            for mirror in range(2):
-                for member in range(2):
-                    block = jnp.zeros((size, LANES), jnp.float32)
-                    for corner in range(4):
-                        r = mirror * 8 + member * 4 + corner
-                        block = jnp.where(place == rows_index[r], rows_weight[r], block)
-                    matrix[start:start + size, pl.ds(wide + (mirror * 2 + member) * LANES, LANES)] = (
-                        block.astype(jnp.bfloat16)
+        done = 0
+        for ring in range(0, rings, 2):
+            for pair in range(4):
+                low, high, lowest = patterns[pair]
+                parts = []
+                for offset in range(2):
+                    first = lowest == ring + offset
+                    second = lowest == ring + offset - 1
+                    for sub in range(0, RING, 8):
+                        parts.append(
+                            jnp.where(first, low[sub:sub + 8], jnp.where(second, high[sub:sub + 8], 0.0))
+                        )
+                matrix[ring * RING:(ring + 2) * RING, pl.ds(wide + pair * LANES, LANES)] = jnp.concatenate(
+                    parts, axis=0
+                ).astype(jnp.bfloat16)
+            ready = (ring + 2) * RING
+            while done < depth and (ready >= done + ROWS or ready == used):
+                size = min(ROWS, depth - done)
+                for mirror in range(2):
+                    members[mirror] = members[mirror] + jnp.dot(
+                        low_t[:, done:done + size],
+                        matrix[done:done + size, pl.ds(wide + mirror * 2 * LANES, 2 * LANES)],
+                        preferred_element_type=jnp.float32,
                     )
-                members[mirror] = members[mirror] + jnp.dot(
-                    low_t[:, start:start + size],
-                    matrix[start:start + size, pl.ds(wide + mirror * 2 * LANES, 2 * LANES)],
-                    preferred_element_type=jnp.float32,
-                )
+                done += size
         values = flat_t[:, lanes]
         coef = nl_pad[:, lanes]
         drive = jnp.maximum(
@@ -121,11 +164,13 @@
         return carry
 
     lax.fori_loop(0, chunks, chunk_step, 0)
-    for start in range(0, padded, ROWS):
-        size = min(ROWS, padded - start)
-        total[start:start + size, :] += jnp.dot(
+    for start in range(0, depth, ROWS):
+        size = min(ROWS, depth - start)
+        spaced[start:start + size, :] = jnp.dot(
             matrix[start:start + size, :], inter[...], preferred_element_type=jnp.float32
         )
+    for ring in range(rings):
+        total[ring * NTH:(ring + 1) * NTH, :] += spaced[ring * RING:ring * RING + NTH, :]
     tiles, halves = owners
     half_bins = count_bins // halves
     for tile in range(tiles):
@@ -143,6 +188,7 @@
 def source_terms(owners, per, spectra, wind, index, weight, nl_coef):
     count_bins, points = spectra.shape
     padded = round_up(count_bins, LANES)
+    depth = round_up(count_bins // NTH * RING, LANES)
     cosine, sine, _ = bin_tables(count_bins)
     tables = np.zeros((2, padded), np.float32)
     tables[0, :count_bins] = cosine
@@ -153,13 +199,14 @@
         functools.partial(source_kernel, owners, per),
         out_shape=jax.ShapeDtypeStruct((group, rows, LANES), jnp.float32),
         scratch_shapes=[
-            pltpu.VMEM((16, padded), jnp.int32),
+            pltpu.VMEM((24, padded), jnp.int32),
             pltpu.VMEM((16, padded), jnp.float32),
             pltpu.VMEM((1, padded), jnp.float32),
+            pltpu.VMEM((depth, points), jnp.float32),
             pltpu.VMEM((points, padded), jnp.float32),
-            pltpu.VMEM((points, padded), jnp.bfloat16),
+            pltpu.VMEM((points, depth), jnp.bfloat16),
             pltpu.VMEM((points, LANES), jnp.float32),
-            pltpu.VMEM((padded, 4 * padded), jnp.bfloat16),
+            pltpu.VMEM((depth, 4 * padded), jnp.bfloat16),
             pltpu.VMEM((4 * padded, points), jnp.bfloat16),
             pltpu.VMEM((padded, points), jnp.float32),
         ],
@@ -287,8 +334,7 @@
     padded = round_up(per, 8)
 
     payload = source_terms(
-        (tiles, halves), per, spectra, wind, dia_index.reshape(16, count_bins),
-        dia_weight.reshape(16, count_bins), nl_coef.reshape(1, count_bins),
+        (tiles, halves), per, spectra, wind, dia_index, dia_weight, nl_coef
     )
     got = lax.all_to_all(payload, ("tile", "bin"), split_axis=0, concat_axis=0, tiled=True)
 

time: 155 us -> 147 us (0.948)
  Pallas kernels: 42.2 us -> 34.5 us
    pallas_call x1, Pallas kernels: 25.8 us -> 18.1 us  [source_terms(): pl.pallas_call(functools.partial(source_kernel, owners, per), out_shape=j...]
    reshape x3 -> x0, local copies, waits for them, and re-layouts: 2.44 us -> none  [the longest x1 0.92 us: shards(): dia_index.reshape(16, count_bins)]
    unnamed x13 -> x19, local copies, waits for them, and re-layouts: 4.22 us -> 6.59 us
where the time goes in v3:
time: 147 us
  blocking collectives  69.5 us (47%)
  Pallas kernels  34.5 us (23%)
  waiting for transfers between devices  27.4 us (19%)
  local copies, waits for them, and re-layouts  7.4 us (5%)
  starting transfers between devices  7.38 us (5%)
    all_to_all x1, blocking collectives, shards(): lax.all_to_all(moved.reshape(tiles, per, columns_tile, latitudes), 'tile'...  69.5 us
    all_to_all x1, waiting for transfers between devices, shards(): lax.all_to_all(payload, ('tile', 'bin'), split_axis=0, concat_axis=0, til...  27.4 us
    pallas_call x1, Pallas kernels, source_terms(): pl.pallas_call(functools.partial(source_kernel, owners, per), out_shape=j...  18.1 us
    pallas_call x1, Pallas kernels, propagate(): pl.pallas_call(functools.partial(propagate_kernel, per, columns_tile, hal...  16.4 us
    all_to_all x1, starting transfers between devices, shards(): lax.all_to_all(payload, ('tile', 'bin'), split_axis=0, concat_axis=0, til...  7.38 us
    unnamed x19, local copies, waits for them, and re-layouts  6.59 us
  transfers between devices with their start and end apart: 1, of which 1 were waited for; matrix products, arithmetic and copies ran while one was open for 1% of the time, Pallas kernels for 0%

profile of v3, /device:TPU:0, one launch (start us, length us, event | category | flops | bytes accessed | tf_op | source)
XLA Modules:
  0.0 146.6 jit_solution(6622926965932234059)
XLA Ops:
  0.0 0.0 copy-start
  0.0 1.3 copy-done
  1.3 0.0 copy-start.1
  1.3 0.9 copy-done.1
  2.2 0.0 copy-start.2
  2.2 0.8 copy-done.2
  3.0 0.0 copy-start.3
  3.0 0.7 copy-done.3
  3.7 0.0 copy-start.4
  3.7 0.7 copy-done.4
  4.4 0.0 copy-start.5
  4.4 0.7 copy-done.5
  5.1 0.0 copy-start.6
  5.1 0.0 copy-start.8
  5.1 0.0 copy-start.7
  5.1 18.1 %source_terms.1 = f32[16,162,128]{2,1,0:T(8,128)} custom-call(f32[1296,256]{1,0:T(8,128)S(1)} %copy-done, f32[2,256]{1,0:T(2,128)S(1)} %copy-done.5, s32[2,2,4,1296]{3,2,1,0:T(4,128)S(1)} %copy-done.1, bf16[2,2,4,1296]{3,2,1,0:T(4,128)(2,1)S(1)} %copy-done.2, f32[1296]{0:T(1024)S(1)} %copy-done.4, f32[2,1408]{1,0:T(2,128)S(1)} %copy-done.3), custom_call_target="tpu_custom_call" | custom-call | tf_op jit(solution)/shard_map/source_terms/pallas_call | solution.py:198
  23.2 7.4 %all-to-all-start = ((f32[16,162,128]{2,1,0:T(8,128)}), f32[16,162,128]{2,1,0:T(8,128)S(1)}, u32[]{:S(2)}, u32[]{:S(2)}) async-start(f32[16,162,128]{2,1,0:T(8,128)} %source_terms.1), calls=%async_computation | async-start | bytes 2752512 | tf_op jit(solution)/shard_map/all_to_all | solution.py:339
  30.6 0.8 dynamic-slice_bitcast_fusion.taps
  31.4 0.0 copy-done.6
  31.4 0.0 copy-done.8
  31.4 0.2 convolution_reduce_fusion
  31.7 0.0 copy-done.7
  31.7 0.1 fusion.3.rel
  31.8 27.4 %all-to-all-done.got = f32[16,162,128]{2,1,0:T(8,128)S(1)} async-done(((f32[16,162,128]{2,1,0:T(8,128)}), f32[16,162,128]{2,1,0:T(8,128)S(1)}, u32[]{:S(2)}, u32[]{:S(2)}) %all-to-all-start) | async-done | bytes 1327136 | tf_op jit(solution)/shard_map/all_to_all | solution.py:339
  59.2 16.4 %propagate.1 = f32[5184,128]{1,0:T(8,128)} custom-call(s32[64]{0:T(128)S(1)} %get-tuple-element.6.base, f32[16,162,128]{2,1,0:T(8,128)S(1)} %all-to-all-done.got, s32[64,128]{1,0:T(8,128)S(1)} %fusion.3.rel, f32[88,128]{1,0:T(8,128)S(1)} %dynamic-slice_bitcast_fusion.taps), custom_call_target="tpu_custom_call" | custom-call | tf_op jit(solution)/shard_map/propagate/pallas_call | solution.py:309
  75.5 69.5 %all_to_all.10 = f32[8,81,8,128]{3,2,1,0:T(8,128)S(1)} all-to-all(f32[8,81,8,128]{3,2,1,0:T(8,128)} %bitcast.10), channel_id=1, replica_groups=mesh['band'=2,'tile'=8,'bin'=2] {'tile'}, dimensions={0} | all-to-all | bytes 5308416 | tf_op jit(solution)/shard_map/all_to_all | solution.py:365
  145.1 1.5 %copy.12 = f32[648,8,128]{2,1,0:T(8,128)} copy(f32[648,8,128]{2,1,0:T(8,128)S(1)} %bitcast.11) | data formatting | bytes 5308416
  (1 shorter events, 0.0 us)
Async XLA Ops:
  0.0 1.3 copy-start
  1.3 0.9 copy-start.1
  2.2 0.8 copy-start.2
  3.0 0.7 copy-start.3
  3.7 0.7 copy-start.4
  4.4 0.7 copy-start.5
  5.1 26.3 %copy-start.6 = (s32[64,128]{1,0:T(8,128)S(1)}, s32[64,128]{1,0:T(8,128)}, u32[]{:S(2)}) copy-start(s32[64,128]{1,0:T(8,128)} %param.12) | copy-start | bytes 98308
  5.1 26.3 %copy-start.8 = (bf16[64,64]{1,0:T(8,128)(2,1)S(1)}, bf16[64,64]{1,0:T(8,128)(2,1)}, u32[]{:S(2)}) copy-start(bf16[64,64]{1,0:T(8,128)(2,1)} %constant.49.clone) | copy-start | bytes 24580
  5.1 26.6 %copy-start.7 = (bf16[128,128]{1,0:T(8,128)(2,1)S(1)}, bf16[128,128]{1,0:T(8,128)(2,1)}, u32[]{:S(2)}) copy-start(bf16[128,128]{1,0:T(8,128)(2,1)} %constant.48.clone) | copy-start | bytes 98308
  23.2 35.9 %all-to-all-start = ((f32[16,162,128]{2,1,0:T(8,128)}), f32[16,162,128]{2,1,0:T(8,128)S(1)}, u32[]{:S(2)}, u32[]{:S(2)}) async-start(f32[16,162,128]{2,1,0:T(8,128)} %source_terms.1), calls=%async_computation | async-start | bytes 2752512 | tf_op jit(solution)/shard_map/all_to_all | solution.py:339

commit v4 on v3

--- a/solution.py
+++ b/solution.py
@@ -1,3 +1,4 @@
+import dataclasses
 import functools
 import math
 
@@ -14,6 +15,8 @@
 LANES = 128
 ROWS = 256
 RING = 40
+COMMON = 192
+SIZES = (160, 176, 192, 208, 224)
 
 LAMBDA = 0.25
 COEF_THREE = (1.0 + LAMBDA) ** (-4)
@@ -45,8 +48,8 @@
     return np.stack([left, here - left, 1.0 + right - here, far - right, -far])
 
 
-def source_kernel(owners, per, spectra, wind, index, weight, nl_coef, tables, out,
-                  code, weight_pad, nl_pad, spaced, flat_t, low_t, wind_t, matrix, inter, total):
+def source_kernel(plan, first_point, spectra, wind, index, weight, nl_coef, tables, out,
+                  code, weight_pad, nl_pad, spaced, flat_t, low_t, wind_t, matrix, inter, total, twice):
     count_bins, points = spectra.shape
     padded = flat_t.shape[1]
     chunks = padded // LANES
@@ -171,21 +174,50 @@
         )
     for ring in range(rings):
         total[ring * NTH:(ring + 1) * NTH, :] += spaced[ring * RING:ring * RING + NTH, :]
-    tiles, halves = owners
-    half_bins = count_bins // halves
-    for tile in range(tiles):
-        for side in range(halves):
-            first = side * half_bins + tile * per
-            valid = min(per, half_bins - tile * per)
-            if valid <= 0:
-                continue
+    pack_payload(plan, first_point, total, out, twice)
+
+
+def pack_payload(plan, first_point, total, out, twice):
+    points = total.shape[1]
+    main, rest, fold = plan.main, plan.rest, plan.fold
+    lane = lax.broadcasted_iota(jnp.int32, (1, LANES), 1)
+    for side in range(plan.halves):
+        for member in range(plan.members):
+            first = side * plan.half_bins + member * plan.per
+            valid = min(main, plan.half_bins - member * plan.per)
+            slot = (side * plan.members + member) % 2
             for half in range(points // LANES):
-                out[tile * halves + side, half * per:half * per + valid, :] = total[
-                    first:first + valid, half * LANES:(half + 1) * LANES
+                values = total[first:first + valid, half * LANES:(half + 1) * LANES]
+                if valid < LANES:
+                    values = jnp.concatenate([values, jnp.zeros((LANES - valid, LANES), jnp.float32)], axis=0)
+                turned = values.T
+                twice[slot, half * LANES:(half + 1) * LANES, :] = turned
+                twice[slot, points + half * LANES:points + (half + 1) * LANES, :] = turned
+            for part in range(plan.parts):
+                owner = (part * plan.members + member) * plan.halves + side
+                begin = first_point[part]
+                out[owner, rest + fold:rest + fold + COMMON, :] = twice[slot, pl.ds(begin, COMMON), :]
+                out[owner, rest + 2 * fold + COMMON:rest + 2 * fold + points, :] = twice[
+                    slot, pl.ds(begin + COMMON, points - COMMON), :
                 ]
-
-
-def source_terms(owners, per, spectra, wind, index, weight, nl_coef):
+                if not rest:
+                    continue
+                shift = lax.rem(begin, LANES)
+                swapped = begin >= LANES
+                near = pltpu.roll(total[first + main:first + main + rest, :LANES], lax.rem(LANES - shift, LANES), 1)
+                away = pltpu.roll(total[first + main:first + main + rest, LANES:], lax.rem(LANES - shift, LANES), 1)
+                keep = (lane < LANES - shift) != swapped
+                lead = jnp.where(keep, near, away)
+                tail = jnp.where(keep, away, near)
+                moved = pltpu.roll(tail, LANES // 2, 1)
+                out[owner, :rest, :] = lead
+                out[owner, rest:rest + fold, :] = jnp.where(lane < LANES // 2, tail[:fold], moved[rest - fold:])
+                out[owner, rest + fold + COMMON:rest + 2 * fold + COMMON, :] = jnp.where(
+                    lane < LANES // 2, moved[:fold], tail[rest - fold:]
+                )
+
+
+def source_terms(plan, first_point, spectra, wind, index, weight, nl_coef):
     count_bins, points = spectra.shape
     padded = round_up(count_bins, LANES)
     depth = round_up(count_bins // NTH * RING, LANES)
@@ -193,11 +225,13 @@
     tables = np.zeros((2, padded), np.float32)
     tables[0, :count_bins] = cosine
     tables[1, :count_bins] = sine
-    group = owners[0] * owners[1]
-    rows = per * (points // LANES)
+    smem = pl.BlockSpec(memory_space=pltpu.SMEM)
+    vmem = pl.BlockSpec(memory_space=pltpu.VMEM)
     return pl.pallas_call(
-        functools.partial(source_kernel, owners, per),
-        out_shape=jax.ShapeDtypeStruct((group, rows, LANES), jnp.float32),
+        functools.partial(source_kernel, plan),
+        out_shape=jax.ShapeDtypeStruct((plan.group, plan.rows(points), LANES), jnp.float32),
+        in_specs=[smem] + [vmem] * 6,
+        out_specs=vmem,
         scratch_shapes=[
             pltpu.VMEM((24, padded), jnp.int32),
             pltpu.VMEM((16, padded), jnp.float32),
@@ -209,22 +243,42 @@
             pltpu.VMEM((depth, 4 * padded), jnp.bfloat16),
             pltpu.VMEM((4 * padded, points), jnp.bfloat16),
             pltpu.VMEM((padded, points), jnp.float32),
+            pltpu.VMEM((2, 2 * points, LANES), jnp.float32),
         ],
         compiler_params=pltpu.CompilerParams(vmem_limit_bytes=52 * 1024 * 1024),
         name="source_terms",
-    )(spectra, wind, index, weight, nl_coef, jnp.asarray(tables))
-
-
-def propagate_kernel(per, columns_tile, halo, base, got, rel, taps, out, ranked, lined, middle, pick, sea):
+    )(first_point, spectra, wind, index, weight, nl_coef, jnp.asarray(tables))
+
+
+def propagate_kernel(plan, slots, base, got, rel, taps, out, ranked, extra, lined, middle, pick, sea):
     group = got.shape[0]
     columns = rel.shape[0]
-    halves = got.shape[1] // per
-    fill = jnp.zeros((LANES - per, LANES), jnp.float32)
+    per, columns_tile, halo = plan.per, plan.columns_tile, plan.halo
+    main, rest, fold = plan.main, plan.rest, plan.fold
+    half_lanes = lax.broadcasted_iota(jnp.int32, (1, LANES), 1) < LANES // 2
+    rest_rows = round_up(rest, 8)
 
     def order(owner, carry):
-        for half in range(halves):
-            values = jnp.concatenate([got[owner, half * per:(half + 1) * per, :], fill], axis=0)
-            ranked[pl.ds(half * LANES * group + owner, LANES, stride=group), :] = values.T
+        common = min(slots, COMMON)
+        ranked[pl.ds(owner, common, stride=group), :] = got[owner, rest + fold:rest + fold + common, :]
+        if slots > COMMON:
+            ranked[pl.ds(owner + COMMON * group, slots - COMMON, stride=group), :] = got[
+                owner, rest + 2 * fold + COMMON:rest + 2 * fold + slots, :
+            ]
+        if rest:
+            lead = got[owner, :rest, :]
+            near = got[owner, rest:rest + fold, :]
+            first = near
+            second = pltpu.roll(near, LANES // 2, 1)
+            if slots > COMMON:
+                away = got[owner, rest + fold + COMMON:rest + 2 * fold + COMMON, :]
+                first = jnp.where(half_lanes, first, pltpu.roll(away, LANES // 2, 1))
+                second = jnp.where(half_lanes, second, away)
+            tail = jnp.concatenate([first[:rest - fold], second], axis=0)
+            fill = jnp.zeros((LANES - rest, LANES), jnp.float32)
+            extra[pl.ds(owner, LANES, stride=group), :] = jnp.concatenate([lead, fill], axis=0).T
+            turned = jnp.concatenate([tail, fill], axis=0).T
+            extra[pl.ds(owner + LANES * group, slots - LANES, stride=group), :] = turned[:slots - LANES]
         return carry
 
     lax.fori_loop(0, group, order, 0, unroll=4)
@@ -234,11 +288,13 @@
 
     def line_up(tile, carry):
         start = pl.multiple_of(tile * LANES, LANES)
-        lined[:, pl.ds(start, LANES)] = ranked[pl.ds(start, LANES), :].T[:padded]
+        lined[:round_up(main, 8), pl.ds(start, LANES)] = ranked[pl.ds(start, LANES), :].T[:round_up(main, 8)]
+        if rest:
+            lined[main:main + rest_rows, pl.ds(start, LANES)] = extra[pl.ds(start, LANES), :].T[:rest_rows]
         return carry
 
     lax.fori_loop(0, rank_tiles, line_up, 0, unroll=4)
-    lined[:, rank_tiles * LANES:] = jnp.zeros((padded, LANES), jnp.float32)
+    lined[:, rank_tiles * LANES:] = jnp.zeros((padded, 2 * LANES), jnp.float32)
 
     for column in range(columns):
         row = jnp.broadcast_to(rel[column:column + 1, :], (8, LANES))
@@ -299,21 +355,21 @@
         bins_step(per // 8 * 8, per % 8)
 
 
-def propagate(per, columns_tile, halo, base, got, rel, taps):
-    group, rows, _ = got.shape
+def propagate(plan, slots, base, got, rel, taps):
     columns = rel.shape[0]
-    points = rows // per * LANES
-    padded = round_up(per, 8)
+    padded = round_up(plan.per, 8)
+    ranks = plan.group * slots
     smem = pl.BlockSpec(memory_space=pltpu.SMEM)
     vmem = pl.BlockSpec(memory_space=pltpu.VMEM)
     return pl.pallas_call(
-        functools.partial(propagate_kernel, per, columns_tile, halo),
-        out_shape=jax.ShapeDtypeStruct(((columns - 2 * halo) * per, LANES), jnp.float32),
+        functools.partial(propagate_kernel, plan, slots),
+        out_shape=jax.ShapeDtypeStruct(((columns - 2 * plan.halo) * plan.per, LANES), jnp.float32),
         in_specs=[smem, vmem, vmem, vmem],
         out_specs=vmem,
         scratch_shapes=[
-            pltpu.VMEM((group * points, LANES), jnp.float32),
-            pltpu.VMEM((padded, group * points + LANES), jnp.float32),
+            pltpu.VMEM((ranks, LANES), jnp.float32),
+            pltpu.VMEM((ranks if plan.rest else 8, LANES), jnp.float32),
+            pltpu.VMEM((padded, ranks + 2 * LANES), jnp.float32),
             pltpu.VMEM((columns, 8, LANES), jnp.float32),
             pltpu.VMEM((columns, 8, LANES), jnp.int32),
             pltpu.VMEM((columns, 8, LANES), jnp.float32),
@@ -323,49 +379,120 @@
     )(base, got, rel, taps)
 
 
+@dataclasses.dataclass(frozen=True)
+class Plan:
+    tiles: int
+    halves: int
+    parts: int
+    half_bins: int
+    columns: int
+
+    @property
+    def group(self):
+        return self.tiles * self.halves
+
+    @property
+    def members(self):
+        return self.tiles // self.parts
+
+    @property
+    def per(self):
+        return -(-self.half_bins // self.members)
+
+    @property
+    def main(self):
+        return min(self.per, LANES)
+
+    @property
+    def rest(self):
+        return self.per - self.main
+
+    @property
+    def fold(self):
+        return -(-self.rest // 2)
+
+    @property
+    def columns_tile(self):
+        return self.columns // self.tiles
+
+    @property
+    def halo(self):
+        return 2 * STEPS if self.parts > 1 else 0
+
+    @property
+    def window(self):
+        return self.columns // self.parts + 2 * self.halo
+
+    def rows(self, slots):
+        return self.rest + (2 if slots > COMMON else 1) * self.fold + slots
+
+
 def shards(spectra, wind, mask, dia_index, dia_weight, nl_coef):
-    count_bins = spectra.shape[0]
-    tiles = lax.axis_size("tile")
-    halves = lax.axis_size("bin")
+    count_bins, points = spectra.shape
     columns, latitudes = mask.shape
-    columns_tile = columns // tiles
-    half_bins = count_bins // halves
-    per = -(-half_bins // tiles)
-    padded = round_up(per, 8)
-
-    payload = source_terms(
-        (tiles, halves), per, spectra, wind, dia_index, dia_weight, nl_coef
+    plan = Plan(
+        tiles=lax.axis_size("tile"), halves=lax.axis_size("bin"), parts=2,
+        half_bins=count_bins // lax.axis_size("bin"), columns=columns,
     )
-    got = lax.all_to_all(payload, ("tile", "bin"), split_axis=0, concat_axis=0, tiled=True)
+    group, members, parts, halo, window = plan.group, plan.members, plan.parts, plan.halo, plan.window
+    sea_total = group * points
+    tile_rank = lax.axis_index("tile")
+
+    ones = mask.astype(jnp.bfloat16)
+    counts = jnp.sum(mask, axis=1)
+    before = jnp.sum(
+        jnp.where(np.tril(np.ones((columns, columns), bool), -1), counts[None, :], 0), axis=1
+    )
+    reach = np.zeros((parts, columns), bool)
+    for part in range(parts):
+        reach[part, (part * (columns // parts) - halo + np.arange(window)) % columns] = True
+    held = jnp.sum(jnp.where(reach, counts[None, :], 0), axis=1)
+    starts = jnp.stack([before[(part * (columns // parts) - halo) % columns] for part in range(parts)])
+    need = -(-(held + starts % group) // group)
+    first_point = jnp.where(need <= points, starts // group, 0)
+    wanted = lax.pmax(jnp.max(need), "band")
+
+    payload = source_terms(plan, first_point, spectra, wind, dia_index, dia_weight, nl_coef)
 
     cosine, sine, speed = bin_tables(count_bins)
     weights = np.concatenate([stencil(speed * cosine), stencil(speed * sine)])
-    table = np.zeros((halves, tiles, padded, LANES), np.float32)
-    for side in range(halves):
-        for tile in range(tiles):
-            valid = max(0, min(per, half_bins - tile * per))
-            begin = side * half_bins + tile * per
-            table[side, tile, :valid, :10] = weights[:, begin:begin + valid].T
+    table = np.zeros((plan.halves, members, round_up(plan.per, 8), LANES), np.float32)
+    for side in range(plan.halves):
+        for member in range(members):
+            valid = max(0, min(plan.per, plan.half_bins - member * plan.per))
+            begin = side * plan.half_bins + member * plan.per
+            table[side, member, :valid, :10] = weights[:, begin:begin + valid].T
     taps = lax.dynamic_slice(
-        jnp.asarray(table),
-        (lax.axis_index("bin"), lax.axis_index("tile"), 0, 0),
-        (1, 1, padded, LANES),
-    ).reshape(padded, LANES)
-
-    ones = mask.astype(jnp.bfloat16)
+        jnp.asarray(table), (lax.axis_index("bin"), tile_rank % members, 0, 0), (1, 1) + table.shape[2:]
+    ).reshape(table.shape[2:])
+
+    part = tile_rank // members
+    begin = (part * (columns // parts) - halo) % columns
     upto = jnp.dot(ones, jnp.asarray(np.triu(np.ones((latitudes, latitudes))), jnp.bfloat16),
-                   preferred_element_type=jnp.float32)
-    before = jnp.dot(jnp.asarray(np.tril(np.ones((columns, columns)), -1), jnp.bfloat16), ones,
-                     preferred_element_type=jnp.float32).sum(axis=1).astype(jnp.int32)
-    total = payload.shape[0] * spectra.shape[1]
-    base = jnp.minimum(before // LANES * LANES, total - LANES)
-    rel = jnp.where(mask == 1, upto.astype(jnp.int32) - 1 + (before - base)[:, None], -1)
-
-    moved = propagate(per, columns_tile, 0, base, got, rel, taps)
+                   preferred_element_type=jnp.float32).astype(jnp.int32)
+    place = (before - first_point[part] * group) % sea_total
+    floor = place // LANES * LANES
+    rel = jnp.where(mask == 1, upto - 1 + (place - floor)[:, None], -1)
+    floor = lax.dynamic_slice(jnp.concatenate([floor, floor]), (begin,), (window,))
+    rel = lax.dynamic_slice(jnp.concatenate([rel, rel]), (begin, 0), (window, latitudes))
+
+    def with_slots(slots):
+        def run(payload, floor, rel, taps):
+            got = lax.all_to_all(
+                payload[:, :plan.rows(slots)], ("tile", "bin"), split_axis=0, concat_axis=0, tiled=True
+            )
+            return propagate(plan, slots, floor, got, rel, taps)
+
+        return run
+
+    sizes = [size for size in SIZES if size < points] + [points]
+    choice = sum((wanted > size).astype(jnp.int32) for size in sizes[:-1])
+    moved = lax.switch(choice, [with_slots(size) for size in sizes], payload, floor, rel, taps)
     result = lax.all_to_all(
-        moved.reshape(tiles, per, columns_tile, latitudes), "tile", split_axis=0, concat_axis=0, tiled=True
-    ).reshape(tiles * per, columns_tile, latitudes)
-    return result[:half_bins]
+        moved.reshape(members, plan.per, plan.columns_tile, latitudes), "tile", split_axis=0, concat_axis=0,
+        axis_index_groups=[list(range(p * members, (p + 1) * members)) for p in range(parts)], tiled=True,
+    ).reshape(members * plan.per, plan.columns_tile, latitudes)
+    return result[:plan.half_bins]
 
 
 def solution(mesh):

time: 147 us -> 156 us (1.061)
  blocking collectives: 69.5 us -> 103 us
  waiting for transfers between devices: 27.4 us -> 0 us
  starting transfers between devices: 7.38 us -> 0 us
  other arithmetic: 0.02 us -> 4.69 us
  between operations: 0.05 us -> 3.97 us
  local copies, waits for them, and re-layouts: 7.4 us -> 8.98 us
    all_to_all x1 -> x0, waiting for transfers between devices: 27.4 us -> none  [shards(): lax.all_to_all(payload, ('tile', 'bin'), split_axis=0, concat_axis=0, til...]
    all_to_all x1 -> x2, blocking collectives: 69.5 us -> 96.8 us  [the longest x1 61.5 us: run(): lax.all_to_all(payload[:, :plan.rows(slots)], ('tile', 'bin'), split_axis...]
    all_to_all x1 -> x0, starting transfers between devices: 7.38 us -> none  [shards(): lax.all_to_all(payload, ('tile', 'bin'), split_axis=0, concat_axis=0, til...]
    pmax x0 -> x1, blocking collectives: none -> 5.82 us  [shards(): wanted = lax.pmax(jnp.max(need), 'band')]
    reduce_sum x0 -> x3, other arithmetic: none -> 2.45 us  [the longest x1 0.86 us: shards(): counts = jnp.sum(mask, axis=1)]
    unnamed x19 -> x13, local copies, waits for them, and re-layouts: 6.59 us -> 6.58 us
  transfers between devices with their start and end apart: 1 -> 0, of which waited for: 1 -> 0; matrix products, arithmetic and copies ran while one was open for 1% -> 0% of each run, Pallas kernels for 0% -> 0%
where the time goes in v4:
time: 156 us; the launch traced here: 157 us
  blocking collectives  103 us (66%)
  Pallas kernels  35.3 us (23%)
  local copies, waits for them, and re-layouts  8.98 us (6%)
  other arithmetic  4.69 us (3%)
  between operations  3.97 us (3%)
    all_to_all x1, blocking collectives, run(): lax.all_to_all(payload[:, :plan.rows(slots)], ('tile', 'bin'), split_axis...  61.5 us
    all_to_all x1, blocking collectives, shards(): lax.all_to_all(moved.reshape(members, plan.per, plan.columns_tile, latitu...  35.3 us
    pallas_call x1, Pallas kernels, source_terms(): pl.pallas_call(functools.partial(source_kernel, plan), out_shape=jax.Shap...  18.1 us
    pallas_call x1, Pallas kernels, propagate(): pl.pallas_call(functools.partial(propagate_kernel, plan, slots), out_shap...  17.2 us
    unnamed x13, local copies, waits for them, and re-layouts  6.58 us
    pmax x1, blocking collectives, shards(): wanted = lax.pmax(jnp.max(need), 'band')  5.82 us

profile of v4, /device:TPU:0, one launch (start us, length us, event | category | flops | bytes accessed | tf_op | source)
XLA Modules:
  0.0 156.9 jit_solution(15407923316585832893)
XLA Ops:
  0.0 0.9 reduce_sum.27
  0.9 0.8 select_reduce_fusion
  1.7 0.8 select_reduce_fusion.1
  2.5 0.7 fusion.13
  3.1 1.4 compare_select_fusion.2
  4.6 0.6 reduce_max.9
  5.2 5.8 %pmax.7 = s32[]{:T(128)} all-reduce(s32[]{:T(128)} %reduce_max.9), channel_id=1, replica_groups=mesh['band'=2,'tile'=8,'bin'=2] {'band'}, use_global_device_ids=true, to_apply=%region_4.5 | all-reduce | flops 1 | bytes 8 | tf_op jit(solution)/shard_map/pmax | solution.py:453
  14.3 0.6 dynamic_slice.12
  15.5 0.1 pad_add_fusion.1
  15.6 0.1 dynamic_slice.13
  15.7 0.9 fusion.3
  16.6 0.1 fusion.4
  16.7 0.9 dynamic-slice_bitcast_fusion
  17.6 0.0 copy-start
  17.6 1.3 copy-done
  18.9 0.0 copy-start.1
  18.9 0.9 copy-done.1
  19.8 0.0 copy-start.2
  19.8 0.8 copy-done.2
  20.6 0.0 copy-start.3
  20.6 0.7 copy-done.3
  21.3 0.0 copy-start.4
  21.3 0.7 copy-done.4
  22.0 0.0 copy-start.5
  22.0 0.7 copy-done.5
  22.7 18.1 %source_terms.1 = f32[16,324,128]{2,1,0:T(8,128)S(1)} custom-call(s32[2]{0:T(128)S(1)} %get-tuple-element.86.first_point, f32[1296,256]{1,0:T(8,128)S(1)} %copy-done, f32[2,256]{1,0:T(2,128)S(1)} %copy-done.5, s32[2,2,4,1296]{3,2,1,0:T(4,128)S(1)} %copy-done.1, bf16[2,2,4,1296]{3,2,1,0:T(4,128)(2,1)S(1)} %copy-done.2, f32[1296]{0:T(1024)S(1)} %copy-done.4, ...), custom_call_target="tpu_custom_call" | custom-call | tf_op jit(solution)/shard_map/source_terms/pallas_call | solution.py:230
  40.8 79.3 %conditional.1 = (f32[5184,128]{1,0:T(8,128)S(1)}) conditional(s32[]{:T(128)} %clamp.3, (f32[16,324,128]{2,1,0:T(8,128)S(1)}, s32[40]{0:T(128)S(1)}, s32[40,128]{1,0:T(8,128)S(1)}, f32[168,128]{1,0:T(8,128)S(1)}) %tuple.23, (f32[16,324,128]{2,1,0:T(8,128)S(1)}, s32[40]{0:T(128)S(1)}, s32[40,128]{1,0:T(8,128)S(1)}, ...), branch_computations={%region_5.6_spmd, %region_6.7_spmd, %region_7.8_spmd, %region_8.9_... | conditional | bytes 9568264 | solution.py:490
  41.0 0.2 slice.18
  41.1 61.5 %all_to_all.33.got = f32[16,292,128]{2,1,0:T(8,128)} all-to-all(f32[16,292,128]{2,1,0:T(8,128)S(1)} %slice.18), channel_id=1, replica_groups=mesh['band'=2,'tile'=8,'bin'=2] {'tile','bin'}, dimensions={0} | all-to-all | bytes 4784128 | tf_op jit(solution)/shard_map/cond/branch_4_fun/all_to_all | solution.py:481
  102.6 17.2 %propagate.10 = f32[5184,128]{1,0:T(8,128)S(1)} custom-call(s32[40]{0:T(128)S(1)} %get-tuple-element.76.base, f32[16,292,128]{2,1,0:T(8,128)} %all_to_all.33.got, s32[40,128]{1,0:T(8,128)S(1)} %get-tuple-element.78.rel, f32[168,128]{1,0:T(8,128)S(1)} %get-tuple-element.79.taps), custom_call_target="tpu_custom_call" | custom-call | tf_op jit(solution)/shard_map/cond/branch_4_fun/propagate/pallas_call | solution.py:364
  120.1 35.3 %all_to_all.35 = f32[4,162,8,128]{3,2,1,0:T(8,128)S(1)} all-to-all(f32[4,162,8,128]{3,2,1,0:T(8,128)S(1)} %bitcast.10), channel_id=1, replica_groups={{0,2,4,6},{8,10,12,14},{1,3,5,7},{9,11,13,15},{16,18,20,22},{24,26,28,3..., dimensions={0} | all-to-all | bytes 5308416 | tf_op jit(solution)/shard_map/all_to_all | solution.py:491
  155.4 1.5 copy.20
  (1 shorter events, 0.0 us)
Async XLA Ops:
  17.6 1.3 copy-start
  18.9 0.9 copy-start.1
  19.8 0.8 copy-start.2
  20.6 0.7 copy-start.3
  21.3 0.7 copy-start.4
  22.0 0.7 copy-start.5

commit v5 on v4

--- a/solution.py
+++ b/solution.py
@@ -16,6 +16,7 @@
 ROWS = 256
 RING = 40
 COMMON = 192
+VMEM_BYTES = 58 * 1024 * 1024
 SIZES = (160, 176, 192, 208, 224)
 
 LAMBDA = 0.25
@@ -48,8 +49,8 @@
     return np.stack([left, here - left, 1.0 + right - here, far - right, -far])
 
 
-def source_kernel(plan, first_point, spectra, wind, index, weight, nl_coef, tables, out,
-                  code, weight_pad, nl_pad, spaced, flat_t, low_t, wind_t, matrix, inter, total, twice):
+def source_kernel(plan, first_point, spectra_far, wind_far, index_far, weight_far, nl_far, tables_far, out,
+                  spectra, wind, index, weight, nl_coef, tables, arrived, code, weight_pad, nl_pad, spaced, flat_t, low_t, wind_t, matrix, inter, total, twice):
     count_bins, points = spectra.shape
     padded = flat_t.shape[1]
     chunks = padded // LANES
@@ -57,10 +58,17 @@
     depth = spaced.shape[0]
     whole = count_bins // LANES
     rest = count_bins - whole * LANES
+    pairs = [(index_far, index), (weight_far, weight), (nl_far, nl_coef), (wind_far, wind),
+             (tables_far, tables), (spectra_far, spectra)]
+    copies = [pltpu.make_async_copy(far, near, arrived.at[k]) for k, (far, near) in enumerate(pairs)]
+    for copy in copies:
+        copy.start()
 
     code[...] = jnp.zeros(code.shape, jnp.int32)
     weight_pad[...] = jnp.zeros(weight_pad.shape, jnp.float32)
     nl_pad[...] = jnp.zeros(nl_pad.shape, jnp.float32)
+    for copy in copies:
+        copy.wait()
     nl_pad[:, :count_bins] = nl_coef[...].reshape(1, count_bins)
     for mirror in range(2):
         for member in range(2):
@@ -167,8 +175,8 @@
         return carry
 
     lax.fori_loop(0, chunks, chunk_step, 0)
-    for start in range(0, depth, ROWS):
-        size = min(ROWS, depth - start)
+    for start in range(0, used, ROWS):
+        size = min(ROWS, used - start)
         spaced[start:start + size, :] = jnp.dot(
             matrix[start:start + size, :], inter[...], preferred_element_type=jnp.float32
         )
@@ -195,7 +203,7 @@
                 twice[slot, points + half * LANES:points + (half + 1) * LANES, :] = turned
             for part in range(plan.parts):
                 owner = (part * plan.members + member) * plan.halves + side
-                begin = first_point[part]
+                begin = lax.rem(first_point[part], points)
                 out[owner, rest + fold:rest + fold + COMMON, :] = twice[slot, pl.ds(begin, COMMON), :]
                 out[owner, rest + 2 * fold + COMMON:rest + 2 * fold + points, :] = twice[
                     slot, pl.ds(begin + COMMON, points - COMMON), :
@@ -227,12 +235,14 @@
     tables[1, :count_bins] = sine
     smem = pl.BlockSpec(memory_space=pltpu.SMEM)
     vmem = pl.BlockSpec(memory_space=pltpu.VMEM)
+    operands = (spectra, wind, index, weight, nl_coef, jnp.asarray(tables))
     return pl.pallas_call(
         functools.partial(source_kernel, plan),
         out_shape=jax.ShapeDtypeStruct((plan.group, plan.rows(points), LANES), jnp.float32),
-        in_specs=[smem] + [vmem] * 6,
+        in_specs=[smem] + [pl.BlockSpec(memory_space=pl.ANY)] * len(operands),
         out_specs=vmem,
-        scratch_shapes=[
+        scratch_shapes=[pltpu.VMEM(operand.shape, operand.dtype) for operand in operands] + [
+            pltpu.SemaphoreType.DMA((len(operands),)),
             pltpu.VMEM((24, padded), jnp.int32),
             pltpu.VMEM((16, padded), jnp.float32),
             pltpu.VMEM((1, padded), jnp.float32),
@@ -245,14 +255,77 @@
             pltpu.VMEM((padded, points), jnp.float32),
             pltpu.VMEM((2, 2 * points, LANES), jnp.float32),
         ],
-        compiler_params=pltpu.CompilerParams(vmem_limit_bytes=52 * 1024 * 1024),
+        compiler_params=pltpu.CompilerParams(vmem_limit_bytes=VMEM_BYTES),
+        cost_estimate=pl.CostEstimate(
+            flops=4 * depth * 4 * padded * points, bytes_accessed=8 * count_bins * points, transcendentals=0
+        ),
         name="source_terms",
-    )(first_point, spectra, wind, index, weight, nl_coef, jnp.asarray(tables))
-
-
-def propagate_kernel(plan, slots, base, got, rel, taps, out, ranked, extra, lined, middle, pick, sea):
+    )(first_point, *operands)
+
+
+def ranks_kernel(plan, sea_total, part, mask, triangle, need, first_point, floor, rel):
+    columns, latitudes = mask.shape
+    sea = mask[...].astype(jnp.float32).astype(jnp.bfloat16)
+
+    def product(left, right):
+        return jnp.dot(left, right, preferred_element_type=jnp.float32)
+
+    upto = product(sea, triangle[...])
+    counts = lax.dot_general(
+        jnp.ones((8, latitudes), jnp.bfloat16), sea, (((1,), (1,)), ((), ())), preferred_element_type=jnp.float32
+    )
+    row = lax.broadcasted_iota(jnp.int32, (columns, columns), 0)
+    col = lax.broadcasted_iota(jnp.int32, (columns, columns), 1)
+    before_row = product(counts.astype(jnp.bfloat16), jnp.where(row < col, 1.0, 0.0).astype(jnp.bfloat16))
+    before_col = jnp.sum(product(jnp.where(col < row, 1.0, 0.0).astype(jnp.bfloat16), sea), axis=1, keepdims=True)
+    lane = lax.broadcasted_iota(jnp.int32, (1, columns), 1)
+    most = 0
+    chosen = 0
+    for p in range(plan.parts):
+        begin = (p * (columns // plan.parts) - plan.halo) % columns
+        inside = (lane + (columns - begin)) & (columns - 1)
+        start = jnp.sum(jnp.where(lane == begin, before_row[:1], 0.0)).astype(jnp.int32)
+        held = jnp.sum(jnp.where(inside < plan.window, counts[:1], 0.0)).astype(jnp.int32)
+        wanted = (held + lax.rem(start, plan.group) + plan.group - 1) // plan.group
+        first = jnp.where(wanted * plan.group <= sea_total, start // plan.group, 0)
+        first_point[p] = first
+        most = jnp.maximum(most, wanted)
+        chosen = jnp.where(part[0] == p, first, chosen)
+    need[0] = most
+
+    def split(before):
+        place = before.astype(jnp.int32) - chosen * plan.group
+        place = jnp.where(place < 0, place + sea_total, place)
+        within = place & (LANES - 1)
+        return place - within, within
+
+    floor[...] = split(before_row[:1])[0]
+    rel[...] = jnp.where(mask[...] == 1, upto.astype(jnp.int32) - 1 + split(before_col)[1], -1)
+
+
+def sea_ranks(plan, sea_total, part, mask):
+    columns, latitudes = mask.shape
+    smem = pl.BlockSpec(memory_space=pltpu.SMEM)
+    vmem = pl.BlockSpec(memory_space=pltpu.VMEM)
+    return pl.pallas_call(
+        functools.partial(ranks_kernel, plan, sea_total),
+        out_shape=[
+            jax.ShapeDtypeStruct((1,), jnp.int32),
+            jax.ShapeDtypeStruct((plan.parts,), jnp.int32),
+            jax.ShapeDtypeStruct((1, columns), jnp.int32),
+            jax.ShapeDtypeStruct((columns, latitudes), jnp.int32),
+        ],
+        in_specs=[smem, vmem, vmem],
+        out_specs=[smem, smem, vmem, vmem],
+        name="sea_ranks",
+    )(part, mask, jnp.asarray(np.triu(np.ones((latitudes, latitudes))), jnp.bfloat16))
+
+
+def propagate_kernel(plan, slots, part, base, got, rel, taps, out, ranked, extra, lined, pick, sea):
     group = got.shape[0]
-    columns = rel.shape[0]
+    columns = plan.window
+    all_columns = rel.shape[0]
+    begin = part[0] * (all_columns // plan.parts) + (all_columns - plan.halo)
     per, columns_tile, halo = plan.per, plan.columns_tile, plan.halo
     main, rest, fold = plan.main, plan.rest, plan.fold
     half_lanes = lax.broadcasted_iota(jnp.int32, (1, LANES), 1) < LANES // 2
@@ -297,7 +370,7 @@
     lined[:, rank_tiles * LANES:] = jnp.zeros((padded, 2 * LANES), jnp.float32)
 
     for column in range(columns):
-        row = jnp.broadcast_to(rel[column:column + 1, :], (8, LANES))
+        row = jnp.broadcast_to(rel[pl.ds(lax.rem(begin + column, all_columns), 1), :], (8, LANES))
         pick[column] = row
         sea[column] = jnp.where(row >= 0, 1.0, 0.0)
 
@@ -313,12 +386,21 @@
             y_taps.append(jnp.where(inside, tap, 0.0))
 
         def expanded(column):
-            start = pl.multiple_of(base[column], LANES)
+            start = pl.multiple_of(base[0, lax.rem(begin + column, all_columns)], LANES)
             chosen = pick[column]
             within = chosen & (LANES - 1)
             low = jnp.take_along_axis(lined[span, pl.ds(start, LANES)], within, axis=1)
             high = jnp.take_along_axis(lined[span, pl.ds(start + LANES, LANES)], within, axis=1)
             return jnp.where(chosen >= LANES, high, low) * sea[column]
+
+        def store(result, column):
+            owner, place = divmod(column - halo, columns_tile)
+            start = (owner * per + first_bin) * columns_tile + place
+            if valid == 8:
+                out[pl.ds(start, 8, stride=columns_tile), :] = result
+            else:
+                for row in range(valid):
+                    out[pl.ds(start + row * columns_tile, 1), :] = result[row:row + 1]
 
         def sweep(values, column):
             value = x_taps[2] * values[2]
@@ -332,19 +414,21 @@
 
         reach = halo // STEPS
         first = {}
+        middle = {}
+
+        def neighbours(values, column):
+            return [values.get((column + k) % columns) for k in range(-2, 3)]
+
+        waiting = list(range(reach, columns - reach))
+        last = list(range(halo, columns - halo))
         for column in range(columns):
             first[column] = expanded(column)
-        for column in range(reach, columns - reach):
-            middle[column] = sweep([first[(column + k) % columns] for k in range(-2, 3)], column)
-        for column in range(halo, columns - halo):
-            result = sweep([middle[(column + k) % columns] for k in range(-2, 3)], column)
-            owner, place = divmod(column - halo, columns_tile)
-            start = (owner * per + first_bin) * columns_tile + place
-            if valid == 8:
-                out[pl.ds(start, 8, stride=columns_tile), :] = result
-            else:
-                for row in range(valid):
-                    out[pl.ds(start + row * columns_tile, 1), :] = result[row:row + 1]
+            for ready in [c for c in waiting if all(v is not None for v in neighbours(first, c))]:
+                middle[ready] = sweep(neighbours(first, ready), ready)
+                waiting.remove(ready)
+            for ready in [c for c in last if all(v is not None for v in neighbours(middle, c))]:
+                store(sweep(neighbours(middle, ready), ready), ready)
+                last.remove(ready)
 
     def full_step(tile, carry):
         bins_step(pl.multiple_of(tile * 8, 8), 8)
@@ -355,8 +439,8 @@
         bins_step(per // 8 * 8, per % 8)
 
 
-def propagate(plan, slots, base, got, rel, taps):
-    columns = rel.shape[0]
+def propagate(plan, slots, part, base, got, rel, taps):
+    columns = plan.window
     padded = round_up(plan.per, 8)
     ranks = plan.group * slots
     smem = pl.BlockSpec(memory_space=pltpu.SMEM)
@@ -364,19 +448,18 @@
     return pl.pallas_call(
         functools.partial(propagate_kernel, plan, slots),
         out_shape=jax.ShapeDtypeStruct(((columns - 2 * plan.halo) * plan.per, LANES), jnp.float32),
-        in_specs=[smem, vmem, vmem, vmem],
+        in_specs=[smem, smem, vmem, vmem, vmem],
         out_specs=vmem,
         scratch_shapes=[
             pltpu.VMEM((ranks, LANES), jnp.float32),
             pltpu.VMEM((ranks if plan.rest else 8, LANES), jnp.float32),
             pltpu.VMEM((padded, ranks + 2 * LANES), jnp.float32),
-            pltpu.VMEM((columns, 8, LANES), jnp.float32),
             pltpu.VMEM((columns, 8, LANES), jnp.int32),
             pltpu.VMEM((columns, 8, LANES), jnp.float32),
         ],
-        compiler_params=pltpu.CompilerParams(vmem_limit_bytes=52 * 1024 * 1024),
+        compiler_params=pltpu.CompilerParams(vmem_limit_bytes=VMEM_BYTES),
         name="propagate",
-    )(base, got, rel, taps)
+    )(part, base, got, rel, taps)
 
 
 @dataclasses.dataclass(frozen=True)
@@ -434,23 +517,19 @@
         tiles=lax.axis_size("tile"), halves=lax.axis_size("bin"), parts=2,
         half_bins=count_bins // lax.axis_size("bin"), columns=columns,
     )
-    group, members, parts, halo, window = plan.group, plan.members, plan.parts, plan.halo, plan.window
-    sea_total = group * points
+    members, parts = plan.members, plan.parts
+    sea_total = plan.group * points
     tile_rank = lax.axis_index("tile")
 
-    ones = mask.astype(jnp.bfloat16)
-    counts = jnp.sum(mask, axis=1)
-    before = jnp.sum(
-        jnp.where(np.tril(np.ones((columns, columns), bool), -1), counts[None, :], 0), axis=1
-    )
-    reach = np.zeros((parts, columns), bool)
-    for part in range(parts):
-        reach[part, (part * (columns // parts) - halo + np.arange(window)) % columns] = True
-    held = jnp.sum(jnp.where(reach, counts[None, :], 0), axis=1)
-    starts = jnp.stack([before[(part * (columns // parts) - halo) % columns] for part in range(parts)])
-    need = -(-(held + starts % group) // group)
-    first_point = jnp.where(need <= points, starts // group, 0)
-    wanted = lax.pmax(jnp.max(need), "band")
+    part = (tile_rank // members).astype(jnp.int32).reshape(1)
+    need, first_point, floor, rel = sea_ranks(plan, sea_total, part, mask)
+    wanted = need
+    bands = lax.axis_size("band")
+    for step in range(1, bands):
+        wanted = jnp.maximum(
+            wanted, lax.ppermute(need, "band", [(band, (band + step) % bands) for band in range(bands)])
+        )
+    wanted = wanted[0]
 
     payload = source_terms(plan, first_point, spectra, wind, dia_index, dia_weight, nl_coef)
 
@@ -466,28 +545,18 @@
         jnp.asarray(table), (lax.axis_index("bin"), tile_rank % members, 0, 0), (1, 1) + table.shape[2:]
     ).reshape(table.shape[2:])
 
-    part = tile_rank // members
-    begin = (part * (columns // parts) - halo) % columns
-    upto = jnp.dot(ones, jnp.asarray(np.triu(np.ones((latitudes, latitudes))), jnp.bfloat16),
-                   preferred_element_type=jnp.float32).astype(jnp.int32)
-    place = (before - first_point[part] * group) % sea_total
-    floor = place // LANES * LANES
-    rel = jnp.where(mask == 1, upto - 1 + (place - floor)[:, None], -1)
-    floor = lax.dynamic_slice(jnp.concatenate([floor, floor]), (begin,), (window,))
-    rel = lax.dynamic_slice(jnp.concatenate([rel, rel]), (begin, 0), (window, latitudes))
-
     def with_slots(slots):
-        def run(payload, floor, rel, taps):
+        def run(payload, part, floor, rel, taps):
             got = lax.all_to_all(
                 payload[:, :plan.rows(slots)], ("tile", "bin"), split_axis=0, concat_axis=0, tiled=True
             )
-            return propagate(plan, slots, floor, got, rel, taps)
+            return propagate(plan, slots, part, floor, got, rel, taps)
 
         return run
 
     sizes = [size for size in SIZES if size < points] + [points]
     choice = sum((wanted > size).astype(jnp.int32) for size in sizes[:-1])
-    moved = lax.switch(choice, [with_slots(size) for size in sizes], payload, floor, rel, taps)
+    moved = lax.switch(choice, [with_slots(size) for size in sizes], payload, part, floor, rel, taps)
     result = lax.all_to_all(
         moved.reshape(members, plan.per, plan.columns_tile, latitudes), "tile", split_axis=0, concat_axis=0,
         axis_index_groups=[list(range(p * members, (p + 1) * members)) for p in range(parts)], tiled=True,

time: 156 us -> 185 us (1.19); the launches traced: 157 us -> 188 us
  Pallas kernels: 35.3 us -> 87.5 us
  blocking collectives: 103 us -> 93.9 us
  local copies, waits for them, and re-layouts: 8.98 us -> 2.55 us
  other arithmetic: 4.69 us -> 0 us
  starting transfers between devices: 0 us -> 3 us
  between operations: 3.97 us -> 1.22 us
    pallas_call x1, Pallas kernels: 17.2 us -> 66.4 us  [propagate(): pl.pallas_call(functools.partial(propagate_kernel, plan, slots), out_shap...]
    pmax x1 -> x0, blocking collectives: 5.82 us -> none  [shards(): wanted = lax.pmax(jnp.max(need), 'band')]
    unnamed x13 -> x1, local copies, waits for them, and re-layouts: 6.58 us -> 1.5 us
    ppermute x0 -> x1, starting transfers between devices: none -> 3 us  [shards(): lax.ppermute(need, 'band', [(band, (band + step) % bands) for band in ran...]
    all_to_all x1, blocking collectives: 61.5 us -> 58.7 us  [run(): lax.all_to_all(payload[:, :plan.rows(slots)], ('tile', 'bin'), split_axis...]
    reduce_sum x3 -> x0, other arithmetic: 2.45 us -> none  [the longest x1 0.86 us: shards(): counts = jnp.sum(mask, axis=1)]
  transfers between devices with their start and end apart: 0 -> 1, of which waited for: 0 -> 0; matrix products, arithmetic and copies ran while one was open for 0% -> 0% of each run, Pallas kernels for 0% -> 10%
where the time goes in v5:
time: 185 us; the launch traced here: 188 us
  blocking collectives  93.9 us (51%)
  Pallas kernels  87.5 us (47%)
  starting transfers between devices  3 us (2%)
  local copies, waits for them, and re-layouts  2.55 us (1%)
    pallas_call x1, Pallas kernels, propagate(): pl.pallas_call(functools.partial(propagate_kernel, plan, slots), out_shap...  66.4 us
    all_to_all x1, blocking collectives, run(): lax.all_to_all(payload[:, :plan.rows(slots)], ('tile', 'bin'), split_axis...  58.7 us
    all_to_all x1, blocking collectives, shards(): lax.all_to_all(moved.reshape(members, plan.per, plan.columns_tile, latitu...  35.2 us
    pallas_call x1, Pallas kernels, source_terms(): pl.pallas_call(functools.partial(source_kernel, plan), out_shape=jax.Shap...  19.4 us
  transfers between devices with their start and end apart: 1, of which 0 were waited for; matrix products, arithmetic and copies ran while one was open for 0% of the time, Pallas kernels for 10%

profile of v5, /device:TPU:0, one launch (start us, length us, event | category | flops | bytes accessed | tf_op | source)
XLA Modules:
  0.0 188.4 jit_solution(14061067829192220949)
XLA Ops:
  0.0 1.7 sea_ranks.1
  1.7 3.0 %collective-permute-start = (s32[1]{0:T(128)}, s32[1]{0:T(128)}, u32[]{:S(2)}, u32[]{:S(2)}) collective-permute-start(s32[1]{0:T(128)} %get-tuple-element.106), channel_id=1, source_target_pairs={{0,16},{16,0},{1,17},{17,1},{2,18},{18,2},{3,19},{19,3},{4,20},{20... | collective-permute-start | bytes 20 | tf_op jit(solution)/shard_map/ppermute | solution.py:530
  4.7 0.9 dynamic-slice_bitcast_fusion
  5.6 19.4 %source_terms.1 = f32[16,324,128]{2,1,0:T(8,128)S(1)} custom-call(s32[2]{0:T(128)} %get-tuple-element.107.first_point, f32[1296,256]{1,0:T(8,128)} %spectra_far.1, f32[2,256]{1,0:T(2,128)} %wind_far.1, s32[2,2,4,1296]{3,2,1,0:T(4,128)} %index_far.1, bf16[2,2,4,1296]{3,2,1,0:T(4,128)(2,1)} %weight_far.1, f32[1296]{0:T(1024)} %nl_far.1, ...), custom_call_target="tpu_custom_call" | custom-call | flops 8858370048 | bytes 2654208 | tf_op jit(solution)/shard_map/source_terms/pallas_call | solution.py:239
  25.1 0.0 collective-permute-done
  26.2 125.5 %conditional.1 = (f32[5184,128]{1,0:T(8,128)S(1)}) conditional(s32[]{:T(128)} %bitcast.1, (f32[16,324,128]{2,1,0:T(8,128)S(1)}, s32[1]{0:T(128)}, s32[1,64]{1,0:T(1,128)S(1)}, s32[64,128]{1,0:T(8,128)S(1)}, f32[168,128]{1,0:T(8,128)S(1)}) %tuple.23, (f32[16,324,128]{2,1,0:T(8,128)S(1)}, s32[1]{0:T(128)}, ...), branch_computations={%region_0.1_spmd, %region_1.2_spmd, %region_2.3_spmd, %region_3.4_... | conditional | bytes 9568264 | solution.py:559
  26.4 0.1 slice.13
  26.6 58.7 %all_to_all.32.got = f32[16,276,128]{2,1,0:T(8,128)} all-to-all(f32[16,276,128]{2,1,0:T(8,128)S(1)} %slice.13), channel_id=1, replica_groups=mesh['band'=2,'tile'=8,'bin'=2] {'tile','bin'}, dimensions={0} | all-to-all | bytes 4521984 | tf_op jit(solution)/shard_map/cond/branch_3_fun/all_to_all | solution.py:550
  85.3 66.4 %propagate.9 = f32[5184,128]{1,0:T(8,128)S(1)} custom-call(s32[1]{0:T(128)} %get-tuple-element.87.part, s32[1,64]{1,0:T(1,128)S(1)} %get-tuple-element.88.base, f32[16,276,128]{2,1,0:T(8,128)} %all_to_all.32.got, s32[64,128]{1,0:T(8,128)S(1)} %get-tuple-element.90.rel, f32[168,128]{1,0:T(8,128)S(1)} %get-tuple-element.91.taps), custom_call_target="tpu_custom_call" | custom-call | tf_op jit(solution)/shard_map/cond/branch_3_fun/propagate/pallas_call | solution.py:448
  151.7 35.2 %all_to_all.35 = f32[4,162,8,128]{3,2,1,0:T(8,128)S(1)} all-to-all(f32[4,162,8,128]{3,2,1,0:T(8,128)S(1)} %bitcast.6), channel_id=1, replica_groups={{0,2,4,6},{8,10,12,14},{1,3,5,7},{9,11,13,15},{16,18,20,22},{24,26,28,3..., dimensions={0} | all-to-all | bytes 5308416 | tf_op jit(solution)/shard_map/all_to_all | solution.py:560
  186.9 1.5 copy.17
Async XLA Ops:
  1.7 23.4 %collective-permute-start = (s32[1]{0:T(128)}, s32[1]{0:T(128)}, u32[]{:S(2)}, u32[]{:S(2)}) collective-permute-start(s32[1]{0:T(128)} %get-tuple-element.106), channel_id=1, source_target_pairs={{0,16},{16,0},{1,17},{17,1},{2,18},{18,2},{3,19},{19,3},{4,20},{20... | collective-permute-start | bytes 20 | tf_op jit(solution)/shard_map/ppermute | solution.py:530

commit v6 on v5

--- a/solution.py
+++ b/solution.py
@@ -17,7 +17,8 @@
 RING = 40
 COMMON = 192
 VMEM_BYTES = 58 * 1024 * 1024
-SIZES = (160, 176, 192, 208, 224)
+SIZES = (160, 176, 192, 208, 224, 240)
+BATCH = 8
 
 LAMBDA = 0.25
 COEF_THREE = (1.0 + LAMBDA) ** (-4)
@@ -331,42 +332,51 @@
     half_lanes = lax.broadcasted_iota(jnp.int32, (1, LANES), 1) < LANES // 2
     rest_rows = round_up(rest, 8)
 
-    def order(owner, carry):
-        common = min(slots, COMMON)
-        ranked[pl.ds(owner, common, stride=group), :] = got[owner, rest + fold:rest + fold + common, :]
+    common = min(slots, COMMON)
+    fill = jnp.zeros((LANES - rest, LANES), jnp.float32)
+
+    def turned_rest(owner):
+        near = got[owner, rest:rest + fold, :]
+        first = near
+        second = pltpu.roll(near, LANES // 2, 1)
         if slots > COMMON:
-            ranked[pl.ds(owner + COMMON * group, slots - COMMON, stride=group), :] = got[
-                owner, rest + 2 * fold + COMMON:rest + 2 * fold + slots, :
-            ]
-        if rest:
-            lead = got[owner, :rest, :]
-            near = got[owner, rest:rest + fold, :]
-            first = near
-            second = pltpu.roll(near, LANES // 2, 1)
+            away = got[owner, rest + fold + COMMON:rest + 2 * fold + COMMON, :]
+            first = jnp.where(half_lanes, first, pltpu.roll(away, LANES // 2, 1))
+            second = jnp.where(half_lanes, second, away)
+        lead = jnp.concatenate([got[owner, :rest, :], fill], axis=0).T
+        return lead, jnp.concatenate([first[:rest - fold], second, fill], axis=0).T
+
+    def order(step, carry):
+        owners = [step * BATCH + k for k in range(BATCH)]
+        turned = [turned_rest(owner) for owner in owners] if rest else []
+        for owner in owners:
+            ranked[pl.ds(owner, common, stride=group), :] = got[owner, rest + fold:rest + fold + common, :]
             if slots > COMMON:
-                away = got[owner, rest + fold + COMMON:rest + 2 * fold + COMMON, :]
-                first = jnp.where(half_lanes, first, pltpu.roll(away, LANES // 2, 1))
-                second = jnp.where(half_lanes, second, away)
-            tail = jnp.concatenate([first[:rest - fold], second], axis=0)
-            fill = jnp.zeros((LANES - rest, LANES), jnp.float32)
-            extra[pl.ds(owner, LANES, stride=group), :] = jnp.concatenate([lead, fill], axis=0).T
-            turned = jnp.concatenate([tail, fill], axis=0).T
-            extra[pl.ds(owner + LANES * group, slots - LANES, stride=group), :] = turned[:slots - LANES]
+                ranked[pl.ds(owner + COMMON * group, slots - COMMON, stride=group), :] = got[
+                    owner, rest + 2 * fold + COMMON:rest + 2 * fold + slots, :
+                ]
+        for owner, (lead, tail) in zip(owners, turned):
+            extra[pl.ds(owner, LANES, stride=group), :] = lead
+            extra[pl.ds(owner + LANES * group, slots - LANES, stride=group), :] = tail[:slots - LANES]
         return carry
 
-    lax.fori_loop(0, group, order, 0, unroll=4)
+    lax.fori_loop(0, group // BATCH, order, 0)
 
     rank_tiles = ranked.shape[0] // LANES
     padded = lined.shape[0]
-
-    def line_up(tile, carry):
-        start = pl.multiple_of(tile * LANES, LANES)
-        lined[:round_up(main, 8), pl.ds(start, LANES)] = ranked[pl.ds(start, LANES), :].T[:round_up(main, 8)]
-        if rest:
-            lined[main:main + rest_rows, pl.ds(start, LANES)] = extra[pl.ds(start, LANES), :].T[:rest_rows]
+    main_rows = round_up(main, 8)
+
+    def line_up(step, carry):
+        starts = [pl.multiple_of(step * (2 * LANES) + k * LANES, LANES) for k in range(2)]
+        turned = [ranked[pl.ds(start, LANES), :].T[:main_rows] for start in starts]
+        more = [extra[pl.ds(start, LANES), :].T[:rest_rows] for start in starts] if rest else []
+        for start, values in zip(starts, turned):
+            lined[:main_rows, pl.ds(start, LANES)] = values
+        for start, values in zip(starts, more):
+            lined[main:main + rest_rows, pl.ds(start, LANES)] = values
         return carry
 
-    lax.fori_loop(0, rank_tiles, line_up, 0, unroll=4)
+    lax.fori_loop(0, rank_tiles // 2, line_up, 0)
     lined[:, rank_tiles * LANES:] = jnp.zeros((padded, 2 * LANES), jnp.float32)
 
     for column in range(columns):
@@ -417,18 +427,17 @@
         middle = {}
 
         def neighbours(values, column):
-            return [values.get((column + k) % columns) for k in range(-2, 3)]
-
-        waiting = list(range(reach, columns - reach))
-        last = list(range(halo, columns - halo))
+            return [values[(column + k) % columns] for k in range(-2, 3)]
+
         for column in range(columns):
             first[column] = expanded(column)
-            for ready in [c for c in waiting if all(v is not None for v in neighbours(first, c))]:
-                middle[ready] = sweep(neighbours(first, ready), ready)
-                waiting.remove(ready)
-            for ready in [c for c in last if all(v is not None for v in neighbours(middle, c))]:
-                store(sweep(neighbours(middle, ready), ready), ready)
-                last.remove(ready)
+        for column in range(reach, columns - reach):
+            middle[column] = sweep(neighbours(first, column), column)
+        results = {}
+        for column in range(halo, columns - halo):
+            results[column] = sweep(neighbours(middle, column), column)
+        for column, result in results.items():
+            store(result, column)
 
     def full_step(tile, carry):
         bins_step(pl.multiple_of(tile * 8, 8), 8)

time: 185 us -> 140 us (0.76); the launches traced: 188 us -> 139 us
  Pallas kernels: 87.5 us -> 38.3 us
    pallas_call x1, Pallas kernels: 66.4 us -> 17.2 us  [propagate(): pl.pallas_call(functools.partial(propagate_kernel, plan, slots), out_shap...]
  transfers between devices with their start and end apart: 1 -> 1, of which waited for: 0 -> 0; matrix products, arithmetic and copies ran while one was open for 0% -> 1% of each run, Pallas kernels for 10% -> 14%
where the time goes in v6:
time: 140 us; the launch traced here: 139 us
  blocking collectives  93.9 us (67%)
  Pallas kernels  38.3 us (27%)
  starting transfers between devices  3 us (2%)
  local copies, waits for them, and re-layouts  2.55 us (2%)
    all_to_all x1, blocking collectives, run(): lax.all_to_all(payload[:, :plan.rows(slots)], ('tile', 'bin'), split_axis...  58.7 us
    all_to_all x1, blocking collectives, shards(): lax.all_to_all(moved.reshape(members, plan.per, plan.columns_tile, latitu...  35.2 us
    pallas_call x1, Pallas kernels, source_terms(): pl.pallas_call(functools.partial(source_kernel, plan), out_shape=jax.Shap...  19.4 us
    pallas_call x1, Pallas kernels, propagate(): pl.pallas_call(functools.partial(propagate_kernel, plan, slots), out_shap...  17.2 us
    ppermute x1, starting transfers between devices, shards(): lax.ppermute(need, 'band', [(band, (band + step) % bands) for band in ran...  3 us
  transfers between devices with their start and end apart: 1, of which 0 were waited for; matrix products, arithmetic and copies ran while one was open for 1% of the time, Pallas kernels for 14%

profile of v6, /device:TPU:0, one launch (start us, length us, event | category | flops | bytes accessed | tf_op | source)
XLA Modules:
  0.0 139.2 jit_solution(4615535125679718739)
XLA Ops:
  0.0 1.7 %sea_ranks.1 = (s32[1]{0:T(128)}, s32[2]{0:T(128)}, s32[1,64]{1,0:T(1,128)S(1)}, s32[64,128]{1,0:T(8,128)S(1)}) custom-call(s32[1]{0:T(128)} %bitcast.part, s32[64,128]{1,0:T(8,128)} %mask.1, bf16[128,128]{1,0:T(8,128)(2,1)} %constant.62.clone.triangle), custom_call_target="tpu_custom_call" | custom-call | tf_op jit(solution)/shard_map/sea_ranks/pallas_call | solution.py:311
  1.7 3.0 %collective-permute-start = (s32[1]{0:T(128)}, s32[1]{0:T(128)}, u32[]{:S(2)}, u32[]{:S(2)}) collective-permute-start(s32[1]{0:T(128)} %get-tuple-element.122), channel_id=1, source_target_pairs={{0,16},{16,0},{1,17},{17,1},{2,18},{18,2},{3,19},{19,3},{4,20},{20... | collective-permute-start | bytes 20 | tf_op jit(solution)/shard_map/ppermute | solution.py:539
  4.7 0.9 dynamic-slice_bitcast_fusion
  5.6 19.4 %source_terms.1 = f32[16,324,128]{2,1,0:T(8,128)S(1)} custom-call(s32[2]{0:T(128)} %get-tuple-element.123.first_point, f32[1296,256]{1,0:T(8,128)} %spectra_far.1, f32[2,256]{1,0:T(2,128)} %wind_far.1, s32[2,2,4,1296]{3,2,1,0:T(4,128)} %index_far.1, bf16[2,2,4,1296]{3,2,1,0:T(4,128)(2,1)} %weight_far.1, f32[1296]{0:T(1024)} %nl_far.1, ...), custom_call_target="tpu_custom_call" | custom-call | flops 8858370048 | bytes 2654208 | tf_op jit(solution)/shard_map/source_terms/pallas_call | solution.py:240
  25.1 0.0 collective-permute-done
  26.2 76.2 %conditional.1 = (f32[5184,128]{1,0:T(8,128)S(1)}) conditional(s32[]{:T(128)} %bitcast.1, (f32[16,324,128]{2,1,0:T(8,128)S(1)}, s32[1]{0:T(128)}, s32[1,64]{1,0:T(1,128)S(1)}, s32[64,128]{1,0:T(8,128)S(1)}, f32[168,128]{1,0:T(8,128)S(1)}) %tuple.26, (f32[16,324,128]{2,1,0:T(8,128)S(1)}, s32[1]{0:T(128)}, ...), branch_computations={%region_0.1_spmd, %region_1.2_spmd, %region_2.3_spmd, %region_3.4_... | conditional | bytes 10092552 | solution.py:568
  26.5 0.1 slice.15
  26.6 58.7 %all_to_all.36.got = f32[16,276,128]{2,1,0:T(8,128)} all-to-all(f32[16,276,128]{2,1,0:T(8,128)S(1)} %slice.15), channel_id=1, replica_groups=mesh['band'=2,'tile'=8,'bin'=2] {'tile','bin'}, dimensions={0} | all-to-all | bytes 4521984 | tf_op jit(solution)/shard_map/cond/branch_3_fun/all_to_all | solution.py:559
  85.3 17.2 %propagate.10 = f32[5184,128]{1,0:T(8,128)S(1)} custom-call(s32[1]{0:T(128)} %get-tuple-element.98.part, s32[1,64]{1,0:T(1,128)S(1)} %get-tuple-element.99.base, f32[16,276,128]{2,1,0:T(8,128)} %all_to_all.36.got, s32[64,128]{1,0:T(8,128)S(1)} %get-tuple-element.101.rel, f32[168,128]{1,0:T(8,128)S(1)} %get-tuple-element.102.taps), custom_call_target="tpu_custom_call" | custom-call | tf_op jit(solution)/shard_map/cond/branch_3_fun/propagate/pallas_call | solution.py:457
  102.5 35.2 %all_to_all.40 = f32[4,162,8,128]{3,2,1,0:T(8,128)S(1)} all-to-all(f32[4,162,8,128]{3,2,1,0:T(8,128)S(1)} %bitcast.6), channel_id=1, replica_groups={{0,2,4,6},{8,10,12,14},{1,3,5,7},{9,11,13,15},{16,18,20,22},{24,26,28,3..., dimensions={0} | all-to-all | bytes 5308416 | tf_op jit(solution)/shard_map/all_to_all | solution.py:569
  137.7 1.5 %copy.18 = f32[648,8,128]{2,1,0:T(8,128)} copy(f32[648,8,128]{2,1,0:T(8,128)S(1)} %bitcast.7) | data formatting | bytes 5308416
Async XLA Ops:
  1.7 23.4 %collective-permute-start = (s32[1]{0:T(128)}, s32[1]{0:T(128)}, u32[]{:S(2)}, u32[]{:S(2)}) collective-permute-start(s32[1]{0:T(128)} %get-tuple-element.122), channel_id=1, source_target_pairs={{0,16},{16,0},{1,17},{17,1},{2,18},{18,2},{3,19},{19,3},{4,20},{20... | collective-permute-start | bytes 20 | tf_op jit(solution)/shard_map/ppermute | solution.py:539

commit v7 on v6

--- a/solution.py
+++ b/solution.py
@@ -51,7 +51,7 @@
 
 
 def source_kernel(plan, first_point, spectra_far, wind_far, index_far, weight_far, nl_far, tables_far, out,
-                  spectra, wind, index, weight, nl_coef, tables, arrived, code, weight_pad, nl_pad, spaced, flat_t, low_t, wind_t, matrix, inter, total, twice):
+                  spectra, wind, index, weight, nl_coef, tables, arrived, code, weight_pad, nl_pad, spaced, flat_t, low_t, matrix, inter, total, twice):
     count_bins, points = spectra.shape
     padded = flat_t.shape[1]
     chunks = padded // LANES
@@ -101,29 +101,25 @@
                     [spectra[whole * LANES:, span], jnp.zeros((LANES - rest, LANES), jnp.float32)], axis=0
                 )
             flat_t[span, lanes] = values.T
-        drive = jnp.concatenate([wind[:, span], jnp.zeros((LANES - 2, LANES), jnp.float32)], axis=0)
-        wind_t[span, :] = drive.T
 
     used = rings * RING
     matrix[used:, :] = jnp.zeros((depth - used, matrix.shape[1]), jnp.bfloat16)
 
-    def chunk_step(chunk, carry):
-        lane = pl.multiple_of(chunk * LANES, LANES)
-        lanes = pl.ds(lane, LANES)
-        wide = pl.multiple_of(chunk * 4 * LANES, 4 * LANES)
+    def members_of(chunk):
+        lanes = slice(chunk * LANES, (chunk + 1) * LANES)
+        wide = chunk * 4 * LANES
         place = lax.broadcasted_iota(jnp.int32, (RING, LANES), 0)
-        nothing = jnp.zeros((RING, LANES), jnp.float32)
         patterns = []
         for pair in range(4):
-            low = nothing
-            high = nothing
+            low = jnp.zeros((RING, LANES), jnp.float32)
+            high = low
             for corner in range(4):
                 r = pair * 4 + corner
-                where = code[pl.ds(r, 1), lanes]
-                amount = jnp.broadcast_to(weight_pad[pl.ds(r, 1), lanes], (RING, LANES))
+                where = code[r:r + 1, lanes]
+                amount = jnp.broadcast_to(weight_pad[r:r + 1, lanes], (RING, LANES))
                 low = jnp.where(place == where, amount, low)
                 high = jnp.where(place + RING == where, amount, high)
-            lowest = jnp.broadcast_to(code[pl.ds(16 + pair, 1), lanes], (8, LANES))
+            lowest = jnp.broadcast_to(code[16 + pair:17 + pair, lanes], (8, LANES))
             patterns.append((low, high, lowest))
         members = [jnp.zeros((points, 2 * LANES), jnp.float32) for _ in range(2)]
         done = 0
@@ -138,25 +134,29 @@
                         parts.append(
                             jnp.where(first, low[sub:sub + 8], jnp.where(second, high[sub:sub + 8], 0.0))
                         )
-                matrix[ring * RING:(ring + 2) * RING, pl.ds(wide + pair * LANES, LANES)] = jnp.concatenate(
-                    parts, axis=0
-                ).astype(jnp.bfloat16)
+                matrix[ring * RING:(ring + 2) * RING, wide + pair * LANES:wide + (pair + 1) * LANES] = (
+                    jnp.concatenate(parts, axis=0).astype(jnp.bfloat16)
+                )
             ready = (ring + 2) * RING
             while done < depth and (ready >= done + ROWS or ready == used):
                 size = min(ROWS, depth - done)
                 for mirror in range(2):
                     members[mirror] = members[mirror] + jnp.dot(
                         low_t[:, done:done + size],
-                        matrix[done:done + size, pl.ds(wide + mirror * 2 * LANES, 2 * LANES)],
+                        matrix[done:done + size, wide + mirror * 2 * LANES:wide + (mirror + 1) * 2 * LANES],
                         preferred_element_type=jnp.float32,
                     )
                 done += size
+        return members
+
+    def interact(chunk, members):
+        lanes = slice(chunk * LANES, (chunk + 1) * LANES)
+        wide = chunk * 4 * LANES
+        valid = min(LANES, count_bins - chunk * LANES)
+        rows = slice(chunk * LANES, chunk * LANES + valid)
         values = flat_t[:, lanes]
         coef = nl_pad[:, lanes]
-        drive = jnp.maximum(
-            wind_t[:, 0:1] * tables[0:1, lanes] + wind_t[:, 1:2] * tables[1:2, lanes], 0.0
-        )
-        base = values + WIND_RATE * drive * values
+        turned = []
         for mirror in range(2):
             third = members[mirror][:, :LANES]
             fourth = members[mirror][:, LANES:]
@@ -164,66 +164,83 @@
                 values * values * (COEF_THREE * third + COEF_FOUR * fourth)
                 - 2.0 * COEF_BOTH * values * third * fourth
             )
-            base = base - 2.0 * interaction
-            for half in range(points // LANES):
-                span = slice(half * LANES, (half + 1) * LANES)
-                turned = interaction[span].T.astype(jnp.bfloat16)
-                for member in range(2):
-                    inter[pl.ds(wide + (mirror * 2 + member) * LANES, LANES), span] = turned
+            turned.append([interaction[half * LANES:(half + 1) * LANES].T for half in range(points // LANES)])
         for half in range(points // LANES):
             span = slice(half * LANES, (half + 1) * LANES)
-            total[lanes, span] = base[span].T
-        return carry
-
-    lax.fori_loop(0, chunks, chunk_step, 0)
+            for mirror in range(2):
+                low = turned[mirror][half].astype(jnp.bfloat16)
+                for member in range(2):
+                    start = wide + (mirror * 2 + member) * LANES
+                    inter[start:start + LANES, span] = low
+            drive = jnp.maximum(
+                wind[0:1, span] * tables[0, rows, :] + wind[1:2, span] * tables[1, rows, :], 0.0
+            )
+            here = spectra[rows, span]
+            both = (turned[0][half] + turned[1][half])[:valid]
+            total[rows, span] = here + WIND_RATE * drive * here - 2.0 * both
+
+    previous = None
+    for chunk in range(chunks):
+        members = members_of(chunk)
+        if previous is not None:
+            interact(chunk - 1, previous)
+        previous = members
+    interact(chunks - 1, previous)
+    added = 0
+    packed = 0
+    owners = [(side, member) for side in range(plan.halves) for member in range(plan.members)]
     for start in range(0, used, ROWS):
         size = min(ROWS, used - start)
         spaced[start:start + size, :] = jnp.dot(
             matrix[start:start + size, :], inter[...], preferred_element_type=jnp.float32
         )
-    for ring in range(rings):
-        total[ring * NTH:(ring + 1) * NTH, :] += spaced[ring * RING:ring * RING + NTH, :]
-    pack_payload(plan, first_point, total, out, twice)
-
-
-def pack_payload(plan, first_point, total, out, twice):
+        while added < rings and added * RING + NTH <= start + size:
+            total[added * NTH:(added + 1) * NTH, :] += spaced[added * RING:added * RING + NTH, :]
+            added += 1
+        while packed < len(owners):
+            side, member = owners[packed]
+            if min(side * plan.half_bins + (member + 1) * plan.per, count_bins) > added * NTH:
+                break
+            pack_payload(plan, first_point, total, out, twice, side, member)
+            packed += 1
+
+
+def pack_payload(plan, first_point, total, out, twice, side, member):
     points = total.shape[1]
     main, rest, fold = plan.main, plan.rest, plan.fold
     lane = lax.broadcasted_iota(jnp.int32, (1, LANES), 1)
-    for side in range(plan.halves):
-        for member in range(plan.members):
-            first = side * plan.half_bins + member * plan.per
-            valid = min(main, plan.half_bins - member * plan.per)
-            slot = (side * plan.members + member) % 2
-            for half in range(points // LANES):
-                values = total[first:first + valid, half * LANES:(half + 1) * LANES]
-                if valid < LANES:
-                    values = jnp.concatenate([values, jnp.zeros((LANES - valid, LANES), jnp.float32)], axis=0)
-                turned = values.T
-                twice[slot, half * LANES:(half + 1) * LANES, :] = turned
-                twice[slot, points + half * LANES:points + (half + 1) * LANES, :] = turned
-            for part in range(plan.parts):
-                owner = (part * plan.members + member) * plan.halves + side
-                begin = lax.rem(first_point[part], points)
-                out[owner, rest + fold:rest + fold + COMMON, :] = twice[slot, pl.ds(begin, COMMON), :]
-                out[owner, rest + 2 * fold + COMMON:rest + 2 * fold + points, :] = twice[
-                    slot, pl.ds(begin + COMMON, points - COMMON), :
-                ]
-                if not rest:
-                    continue
-                shift = lax.rem(begin, LANES)
-                swapped = begin >= LANES
-                near = pltpu.roll(total[first + main:first + main + rest, :LANES], lax.rem(LANES - shift, LANES), 1)
-                away = pltpu.roll(total[first + main:first + main + rest, LANES:], lax.rem(LANES - shift, LANES), 1)
-                keep = (lane < LANES - shift) != swapped
-                lead = jnp.where(keep, near, away)
-                tail = jnp.where(keep, away, near)
-                moved = pltpu.roll(tail, LANES // 2, 1)
-                out[owner, :rest, :] = lead
-                out[owner, rest:rest + fold, :] = jnp.where(lane < LANES // 2, tail[:fold], moved[rest - fold:])
-                out[owner, rest + fold + COMMON:rest + 2 * fold + COMMON, :] = jnp.where(
-                    lane < LANES // 2, moved[:fold], tail[rest - fold:]
-                )
+    first = side * plan.half_bins + member * plan.per
+    valid = min(main, plan.half_bins - member * plan.per)
+    slot = (side * plan.members + member) % 2
+    for half in range(points // LANES):
+        values = total[first:first + valid, half * LANES:(half + 1) * LANES]
+        if valid < LANES:
+            values = jnp.concatenate([values, jnp.zeros((LANES - valid, LANES), jnp.float32)], axis=0)
+        turned = values.T
+        twice[slot, half * LANES:(half + 1) * LANES, :] = turned
+        twice[slot, points + half * LANES:points + (half + 1) * LANES, :] = turned
+    for part in range(plan.parts):
+        owner = (part * plan.members + member) * plan.halves + side
+        begin = lax.rem(first_point[part], points)
+        out[owner, rest + fold:rest + fold + COMMON, :] = twice[slot, pl.ds(begin, COMMON), :]
+        out[owner, rest + 2 * fold + COMMON:rest + 2 * fold + points, :] = twice[
+            slot, pl.ds(begin + COMMON, points - COMMON), :
+        ]
+        if not rest:
+            continue
+        shift = lax.rem(begin, LANES)
+        swapped = begin >= LANES
+        near = pltpu.roll(total[first + main:first + main + rest, :LANES], lax.rem(LANES - shift, LANES), 1)
+        away = pltpu.roll(total[first + main:first + main + rest, LANES:], lax.rem(LANES - shift, LANES), 1)
+        keep = (lane < LANES - shift) != swapped
+        lead = jnp.where(keep, near, away)
+        tail = jnp.where(keep, away, near)
+        moved = pltpu.roll(tail, LANES // 2, 1)
+        out[owner, :rest, :] = lead
+        out[owner, rest:rest + fold, :] = jnp.where(lane < LANES // 2, tail[:fold], moved[rest - fold:])
+        out[owner, rest + fold + COMMON:rest + 2 * fold + COMMON, :] = jnp.where(
+            lane < LANES // 2, moved[:fold], tail[rest - fold:]
+        )
 
 
 def source_terms(plan, first_point, spectra, wind, index, weight, nl_coef):
@@ -231,9 +248,7 @@
     padded = round_up(count_bins, LANES)
     depth = round_up(count_bins // NTH * RING, LANES)
     cosine, sine, _ = bin_tables(count_bins)
-    tables = np.zeros((2, padded), np.float32)
-    tables[0, :count_bins] = cosine
-    tables[1, :count_bins] = sine
+    tables = np.stack([cosine, sine]).astype(np.float32)[:, :, None] * np.ones((1, 1, LANES), np.float32)
     smem = pl.BlockSpec(memory_space=pltpu.SMEM)
     vmem = pl.BlockSpec(memory_space=pltpu.VMEM)
     operands = (spectra, wind, index, weight, nl_coef, jnp.asarray(tables))
@@ -250,7 +265,6 @@
             pltpu.VMEM((depth, points), jnp.float32),
             pltpu.VMEM((points, padded), jnp.float32),
             pltpu.VMEM((points, depth), jnp.bfloat16),
-            pltpu.VMEM((points, LANES), jnp.float32),
             pltpu.VMEM((depth, 4 * padded), jnp.bfloat16),
             pltpu.VMEM((4 * padded, points), jnp.bfloat16),
             pltpu.VMEM((padded, points), jnp.float32),
@@ -322,7 +336,7 @@
     )(part, mask, jnp.asarray(np.triu(np.ones((latitudes, latitudes))), jnp.bfloat16))
 
 
-def propagate_kernel(plan, slots, part, base, got, rel, taps, out, ranked, extra, lined, pick, sea):
+def propagate_kernel(plan, slots, part, base, got, rel, taps, out, ranked, extra, lined, pick, sea, starts):
     group = got.shape[0]
     columns = plan.window
     all_columns = rel.shape[0]
@@ -380,7 +394,9 @@
     lined[:, rank_tiles * LANES:] = jnp.zeros((padded, 2 * LANES), jnp.float32)
 
     for column in range(columns):
-        row = jnp.broadcast_to(rel[pl.ds(lax.rem(begin + column, all_columns), 1), :], (8, LANES))
+        source = (begin + column) & (all_columns - 1)
+        starts[column] = base[0, source]
+        row = jnp.broadcast_to(rel[pl.ds(source, 1), :], (8, LANES))
         pick[column] = row
         sea[column] = jnp.where(row >= 0, 1.0, 0.0)
 
@@ -396,7 +412,7 @@
             y_taps.append(jnp.where(inside, tap, 0.0))
 
         def expanded(column):
-            start = pl.multiple_of(base[0, lax.rem(begin + column, all_columns)], LANES)
+            start = pl.multiple_of(starts[column], LANES)
             chosen = pick[column]
             within = chosen & (LANES - 1)
             low = jnp.take_along_axis(lined[span, pl.ds(start, LANES)], within, axis=1)
@@ -465,6 +481,7 @@
             pltpu.VMEM((padded, ranks + 2 * LANES), jnp.float32),
             pltpu.VMEM((columns, 8, LANES), jnp.int32),
             pltpu.VMEM((columns, 8, LANES), jnp.float32),
+            pltpu.SMEM((columns,), jnp.int32),
         ],
         compiler_params=pltpu.CompilerParams(vmem_limit_bytes=VMEM_BYTES),
         name="propagate",

time: 140 us -> 129 us (0.921)
  blocking collectives: 93.9 us -> 87.6 us
  Pallas kernels: 38.3 us -> 33.5 us
    all_to_all x1, blocking collectives: 58.7 us -> 52 us  [run(): lax.all_to_all(payload[:, :plan.rows(slots)], ('tile', 'bin'), split_axis...]
    pallas_call x1, Pallas kernels: 19.4 us -> 15.2 us  [source_terms(): pl.pallas_call(functools.partial(source_kernel, plan), out_shape=jax.Shap...]
  transfers between devices with their start and end apart: 1 -> 1, of which waited for: 0 -> 0; matrix products, arithmetic and copies ran while one was open for 1% -> 1% of each run, Pallas kernels for 14% -> 12%
where the time goes in v7:
time: 129 us; the launch traced here: 128 us
  blocking collectives  87.6 us (68%)
  Pallas kernels  33.5 us (26%)
  starting transfers between devices  3 us (2%)
  local copies, waits for them, and re-layouts  2.53 us (2%)
    all_to_all x1, blocking collectives, run(): lax.all_to_all(payload[:, :plan.rows(slots)], ('tile', 'bin'), split_axis...  52 us
    all_to_all x1, blocking collectives, shards(): lax.all_to_all(moved.reshape(members, plan.per, plan.columns_tile, latitu...  35.5 us
    pallas_call x1, Pallas kernels, propagate(): pl.pallas_call(functools.partial(propagate_kernel, plan, slots), out_shap...  16.7 us
    pallas_call x1, Pallas kernels, source_terms(): pl.pallas_call(functools.partial(source_kernel, plan), out_shape=jax.Shap...  15.2 us
    ppermute x1, starting transfers between devices, shards(): lax.ppermute(need, 'band', [(band, (band + step) % bands) for band in ran...  3 us
  transfers between devices with their start and end apart: 1, of which 0 were waited for; matrix products, arithmetic and copies ran while one was open for 1% of the time, Pallas kernels for 12%

profile of v7, /device:TPU:0, one launch (start us, length us, event | category | flops | bytes accessed | tf_op | source)
XLA Modules:
  0.0 128.3 jit_solution(5242363515393065382)
XLA Ops:
  0.0 1.7 %sea_ranks.1 = (s32[1]{0:T(128)}, s32[2]{0:T(128)}, s32[1,64]{1,0:T(1,128)S(1)}, s32[64,128]{1,0:T(8,128)S(1)}) custom-call(s32[1]{0:T(128)} %bitcast.part, s32[64,128]{1,0:T(8,128)} %mask.1, bf16[128,128]{1,0:T(8,128)(2,1)} %constant.62.clone.triangle), custom_call_target="tpu_custom_call" | custom-call | tf_op jit(solution)/shard_map/sea_ranks/pallas_call | solution.py:325
  1.7 3.0 %collective-permute-start = (s32[1]{0:T(128)}, s32[1]{0:T(128)}, u32[]{:S(2)}, u32[]{:S(2)}) collective-permute-start(s32[1]{0:T(128)} %get-tuple-element.122), channel_id=1, source_target_pairs={{0,16},{16,0},{1,17},{17,1},{2,18},{18,2},{3,19},{19,3},{4,20},{20... | collective-permute-start | bytes 20 | tf_op jit(solution)/shard_map/ppermute | solution.py:556
  4.7 0.9 dynamic-slice_bitcast_fusion
  5.6 15.2 %source_terms.1 = f32[16,324,128]{2,1,0:T(8,128)S(1)} custom-call(s32[2]{0:T(128)} %get-tuple-element.123.first_point, f32[1296,256]{1,0:T(8,128)} %spectra_far.1, f32[2,256]{1,0:T(2,128)} %wind_far.1, s32[2,2,4,1296]{3,2,1,0:T(4,128)} %index_far.1, bf16[2,2,4,1296]{3,2,1,0:T(4,128)(2,1)} %weight_far.1, f32[1296]{0:T(1024)} %nl_far.1, ...), custom_call_target="tpu_custom_call" | custom-call | flops 8858370048 | bytes 2654208 | tf_op jit(solution)/shard_map/source_terms/pallas_call | solution.py:255
  20.8 0.0 collective-permute-done
  22.0 69.3 %conditional.1 = (f32[5184,128]{1,0:T(8,128)S(1)}) conditional(s32[]{:T(128)} %bitcast.1, (f32[16,324,128]{2,1,0:T(8,128)S(1)}, s32[1]{0:T(128)}, s32[1,64]{1,0:T(1,128)S(1)}, s32[64,128]{1,0:T(8,128)S(1)}, f32[168,128]{1,0:T(8,128)S(1)}) %tuple.26, (f32[16,324,128]{2,1,0:T(8,128)S(1)}, s32[1]{0:T(128)}, ...), branch_computations={%region_0.1_spmd, %region_1.2_spmd, %region_2.3_spmd, %region_3.4_... | conditional | bytes 10092552 | solution.py:585
  22.2 0.1 slice.14
  22.4 52.0 %all_to_all.35.got = f32[16,243,128]{2,1,0:T(8,128)} all-to-all(f32[16,243,128]{2,1,0:T(8,128)S(1)} %slice.14), channel_id=1, replica_groups=mesh['band'=2,'tile'=8,'bin'=2] {'tile','bin'}, dimensions={0} | all-to-all | bytes 3981312 | tf_op jit(solution)/shard_map/cond/branch_2_fun/all_to_all | solution.py:576
  74.4 16.7 %propagate.9 = f32[5184,128]{1,0:T(8,128)S(1)} custom-call(s32[1]{0:T(128)} %get-tuple-element.93.part, s32[1,64]{1,0:T(1,128)S(1)} %get-tuple-element.94.base, f32[16,243,128]{2,1,0:T(8,128)} %all_to_all.35.got, s32[64,128]{1,0:T(8,128)S(1)} %get-tuple-element.96.rel, f32[168,128]{1,0:T(8,128)S(1)} %get-tuple-element.97.taps), custom_call_target="tpu_custom_call" | custom-call | tf_op jit(solution)/shard_map/cond/branch_2_fun/propagate/pallas_call | solution.py:473
  91.3 35.5 %all_to_all.40 = f32[4,162,8,128]{3,2,1,0:T(8,128)S(1)} all-to-all(f32[4,162,8,128]{3,2,1,0:T(8,128)S(1)} %bitcast.6), channel_id=1, replica_groups={{0,2,4,6},{8,10,12,14},{1,3,5,7},{9,11,13,15},{16,18,20,22},{24,26,28,3..., dimensions={0} | all-to-all | bytes 5308416 | tf_op jit(solution)/shard_map/all_to_all | solution.py:586
  126.8 1.5 %copy.18 = f32[648,8,128]{2,1,0:T(8,128)} copy(f32[648,8,128]{2,1,0:T(8,128)S(1)} %bitcast.7) | data formatting | bytes 5308416
Async XLA Ops:
  1.7 19.1 %collective-permute-start = (s32[1]{0:T(128)}, s32[1]{0:T(128)}, u32[]{:S(2)}, u32[]{:S(2)}) collective-permute-start(s32[1]{0:T(128)} %get-tuple-element.122), channel_id=1, source_target_pairs={{0,16},{16,0},{1,17},{17,1},{2,18},{18,2},{3,19},{19,3},{4,20},{20... | collective-permute-start | bytes 20 | tf_op jit(solution)/shard_map/ppermute | solution.py:556
